TPU v7x, 128 devices: a whole 4x4x4 slice. The times are simulated.
128 devices in a mesh: sp: 16 (over z, y), tp: 8 (over x, core).
Axes of the slice: x: 4, y: 4, z: 4, core: 2. Of those that a mesh axis runs over, the one named last changes fastest.
Arguments:
- tokens: bfloat16 [8192, 5120], P('sp', 'tp'), may hold values from -6 to 6
- w_query: bfloat16 [5120, 5120], P(None, 'tp'), may hold values from -0.078125 to 0.078125
- w_key: bfloat16 [5120, 5120], P(None, 'tp'), may hold values from -0.078125 to 0.078125
- w_value: bfloat16 [5120, 5120], P(None, 'tp'), may hold values from -0.078125 to 0.078125
- cache_keys: bfloat16 [64, 128, 5120], P('sp', None, 'tp'), may hold values from -256 to 256, as said below
- cache_values: bfloat16 [64, 128, 5120], P('sp', None, 'tp'), may hold values from -6 to 6
- tile_level: int32 [64], P('sp'), may hold values from 0 to 2
- window_map: int32 [16, 8], replicated, may hold values from 0 to 63, as said below
Outputs:
- attended: bfloat16 [8192, 5120], P('sp', 'tp')
Inputs may be any that keep to these rules, and one draw needn't show every extreme that they name: `window_map`: row d lists 8 blocks held by 8 different indices of sp, one block from each; block b is held by index b // 4. `cache_keys`: cached keys mostly of order one.
All inputs are finite; a program needn't handle non-finite values.
Results may differ from a plain program's by a relative error of at most 0.0079.
Values may be sent and summed in bfloat16 or wider, within the bound.
A program may use at most 128 MiB of HBM per device.

v0:
```python
import math

import jax
import jax.numpy as jnp
from jax import lax
from jax.sharding import PartitionSpec as P

HD = 128
TILE = 128


def with_halo(array, sides, width):
    for axis, dim in sides:
        count, length = (lax.axis_size(axis), array.shape[dim])
        up = [(i, (i + 1) % count) for i in range(count - 1)]
        down = [(j, i) for i, j in up]
        last = lax.slice_in_dim(array, length - width, length, axis=dim)
        first = lax.slice_in_dim(array, 0, width, axis=dim)
        before = lax.ppermute(last, axis, up)
        after = lax.ppermute(first, axis, down)
        array = jnp.concatenate([before, array, after], axis=dim)
    return array


def body(tokens, w_query, w_key, w_value, cache_keys, cache_values, tile_level, window_map):
    tok_rows = tokens.shape[0]
    local_width = w_query.shape[1]
    gathered = lax.all_gather(tokens, "tp", axis=1, tiled=True)
    query_rows = jnp.dot(gathered, w_query, preferred_element_type=jnp.float32).astype(jnp.bfloat16)
    key_rows = jnp.dot(gathered, w_key, preferred_element_type=jnp.float32).astype(jnp.bfloat16)
    value_rows = jnp.dot(gathered, w_value, preferred_element_type=jnp.float32).astype(jnp.bfloat16)
    stacked = jnp.stack([key_rows, value_rows])
    extended = with_halo(stacked, (("sp", 1),), tok_rows)
    band_keys = extended[0]
    band_values = extended[1]
    own_index = lax.axis_index("sp")
    device_count = lax.axis_size("sp")
    blocks_held = cache_keys.shape[0]
    holder_of = window_map // blocks_held
    local_of = window_map % blocks_held
    own_row = lax.dynamic_index_in_dim(window_map, own_index, 0, keepdims=False)
    matches = holder_of == own_index
    wanted = jnp.any(matches, axis=1)
    local_pick = jnp.sum(jnp.where(matches, local_of, 0), axis=1)
    send_keys = jnp.where(
        wanted[:, None, None], jnp.take(cache_keys, local_pick, axis=0), jnp.zeros((), jnp.bfloat16)
    )
    send_values = jnp.where(
        wanted[:, None, None],
        jnp.take(cache_values, local_pick, axis=0),
        jnp.zeros((), jnp.bfloat16),
    )
    received_keys, received_values = (
        lax.all_to_all(send_keys, "sp", split_axis=0, concat_axis=0, tiled=True),
        lax.all_to_all(send_values, "sp", split_axis=0, concat_axis=0, tiled=True),
    )
    own_holders = own_row // blocks_held
    fetched_keys = jnp.take(received_keys, own_holders, axis=0).reshape(-1, local_width)
    fetched_values = jnp.take(received_values, own_holders, axis=0).reshape(-1, local_width)
    token_levels = jnp.repeat(tile_level, TILE)
    radius = (token_levels + 1) * tok_rows // 3
    query_pos = own_index * tok_rows + jnp.arange(tok_rows, dtype=jnp.int32)
    key_pos = (own_index - 1) * tok_rows + jnp.arange(3 * tok_rows, dtype=jnp.int32)
    distance = jnp.abs(key_pos[None, :] - query_pos[:, None])
    allowed = (
        (distance <= radius[:, None])
        & (key_pos[None, :] >= 0)
        & (key_pos[None, :] < device_count * tok_rows)
    )
    score_scale = 1.0 / math.sqrt(HD)
    contract = (((1,), (1,)), ((), ()))
    outputs = []
    for head_index in range(local_width // HD):
        low = head_index * HD
        query_head = query_rows[:, low : low + HD]
        band_scores = (
            lax.dot_general(
                query_head,
                band_keys[:, low : low + HD],
                contract,
                preferred_element_type=jnp.float32,
            )
            * score_scale
        )
        band_scores = jnp.where(allowed, band_scores, -jnp.inf)
        cache_scores = (
            lax.dot_general(
                query_head,
                fetched_keys[:, low : low + HD],
                contract,
                preferred_element_type=jnp.float32,
            )
            * score_scale
        )
        largest = jnp.maximum(jnp.max(band_scores, axis=1), jnp.max(cache_scores, axis=1))[:, None]
        band_weights = jnp.exp(band_scores - largest)
        cache_weights = jnp.exp(cache_scores - largest)
        total = jnp.sum(band_weights, axis=1) + jnp.sum(cache_weights, axis=1)
        mixed = jnp.dot(
            band_weights.astype(jnp.bfloat16),
            band_values[:, low : low + HD],
            preferred_element_type=jnp.float32,
        )
        mixed = mixed + jnp.dot(
            cache_weights.astype(jnp.bfloat16),
            fetched_values[:, low : low + HD],
            preferred_element_type=jnp.float32,
        )
        outputs.append((mixed / total[:, None]).astype(jnp.bfloat16))
    return jnp.concatenate(outputs, axis=1)


def solution(mesh):
    placed = (
        P("sp", "tp"),
        P(None, "tp"),
        P(None, "tp"),
        P(None, "tp"),
        P("sp", None, "tp"),
        P("sp", None, "tp"),
        P("sp"),
        P(),
    )
    return jax.shard_map(body, mesh=mesh, in_specs=placed, out_specs=P("sp", "tp"), check_vma=False)
```

profile of v0, /device:TPU:0, one launch (start us, length us, event | category | flops | bytes accessed | tf_op | source)
XLA Modules:
  0.0 184.0 jit_solution(3693034703065123947)
XLA Ops:
  8.7 2.4 %gather_fusion.2 = bf16[16,128,640]{2,1,0:T(8,128)(2,1)} fusion(bf16[4,128,640]{2,1,0:T(8,128)(2,1)S(1)} %copy-done, s32[1024]{0:T(1024)S(1)} %pad_clamp_fusion.1), kind=kCustom, calls=%fused_computation.2.clone | custom fusion | bytes 5242944 | tf_op jit(solution)/shard_map/jit(_take)/gather | solution.py:50
  11.2 2.4 %gather_fusion = bf16[16,128,640]{2,1,0:T(8,128)(2,1)} fusion(bf16[4,128,640]{2,1,0:T(8,128)(2,1)S(1)} %copy-done.2, s32[1024]{0:T(1024)S(1)} %pad_clamp_fusion.1), kind=kCustom, calls=%fused_computation.clone | custom fusion | bytes 5242944 | tf_op jit(solution)/shard_map/jit(_take)/gather | solution.py:46
  13.5 4.9 %select_select_fusion = (bf16[16,128,640]{2,1,0:T(8,128)(2,1)S(1)}, bf16[16,128,640]{2,1,0:T(8,128)(2,1)}) fusion(bf16[16,128,640]{2,1,0:T(8,128)(2,1)} %gather_fusion.2, pred[16]{0:T(512)(128)(4,1)S(1)} %compare_and_fusion.1, pred[16]{0:T(512)(128)(4,1)S(1)} %get-tuple-element.9, bf16[16,128,640]{2,1,0:T(8,128)(2,1)} %gather_fusion), kind=kLoop, calls=%fused_computation.33 | loop fusion | flops 5242880 | bytes 10485792 | tf_op jit(solution)/shard_map/jit(_where)/select_n | solution.py:48
  18.5 42.0 %all_to_all.10 = bf16[16,128,640]{2,1,0:T(8,128)(2,1)} all-to-all(bf16[16,128,640]{2,1,0:T(8,128)(2,1)S(1)} %get-tuple-element.13), channel_id=1, replica_groups=mesh['sp'=16,'tp'=8] {'sp'}, dimensions={0} | all-to-all | bytes 5242880 | tf_op jit(solution)/shard_map/all_to_all | solution.py:55
  60.5 3.9 %all-to-all-start = ((bf16[16,128,640]{2,1,0:T(8,128)(2,1)}), bf16[16,128,640]{2,1,0:T(8,128)(2,1)S(1)}, u32[]{:S(2)}, u32[]{:S(2)}) async-start(bf16[16,128,640]{2,1,0:T(8,128)(2,1)} %get-tuple-element.14), calls=%async_computation | async-start | bytes 5242880 | tf_op jit(solution)/shard_map/all_to_all | solution.py:54
  64.7 3.5 %gather_fusion.3 = bf16[8,128,640]{2,1,0:T(8,128)(2,1)} fusion(bf16[16,128,640]{2,1,0:T(8,128)(2,1)} %all_to_all.10, s32[1024]{0:T(1024)S(1)} %pad_clamp_fusion), kind=kCustom, calls=%fused_computation.3.clone | custom fusion | bytes 2621472 | tf_op jit(solution)/shard_map/jit(_take)/gather | solution.py:59
  68.3 32.6 %all-to-all-done = bf16[16,128,640]{2,1,0:T(8,128)(2,1)S(1)} async-done(((bf16[16,128,640]{2,1,0:T(8,128)(2,1)}), bf16[16,128,640]{2,1,0:T(8,128)(2,1)S(1)}, u32[]{:S(2)}, u32[]{:S(2)}) %all-to-all-start) | async-done | bytes 2621472 | tf_op jit(solution)/shard_map/all_to_all | solution.py:54
  100.9 1.8 gather_fusion.1
  102.7 2.0 %broadcast_select_fusion = (bf16[8,128,640]{2,1,0:T(8,128)(2,1)S(1)}, bf16[8,128,640]{2,1,0:T(8,128)(2,1)S(1)}) fusion(bf16[8,128,640]{2,1,0:T(8,128)(2,1)} %gather_fusion.3, pred[8]{0:T(512)(128)(4,1)S(1)} %get-tuple-element.6, bf16[8,128,640]{2,1,0:T(8,128)(2,1)} %gather_fusion.1), kind=kLoop, calls=%fused_computation.71 | loop fusion | flops 1310720 | bytes 5242888 | tf_op jit(solution)/shard_map/jit(_take)/select_n | solution.py:59
  104.8 8.8 %fusion.43 = bf16[1,512,640]{2,1,0:T(8,128)(2,1)S(1)} fusion(bf16[512,5120]{1,0:T(8,128)(2,1)} %all-gather.2.cloned.1.call-done, bf16[5120,640]{1,0:T(8,128)(2,1)} %param.15), kind=kOutput, calls=%fused_computation.74 | convolution fusion | flops 3355770880 | bytes 12451840 | tf_op jit(solution)/shard_map/dot_general | solution.py:31
  113.6 6.6 %fusion.42 = bf16[1,512,640]{2,1,0:T(8,128)(2,1)S(1)} fusion(bf16[512,5120]{1,0:T(8,128)(2,1)S(1)} %copy-done.4, bf16[5120,640]{1,0:T(8,128)(2,1)} %param.14), kind=kOutput, calls=%fused_computation.73 | convolution fusion | flops 3355770880 | bytes 12451840 | tf_op jit(solution)/shard_map/dot_general | solution.py:30
  120.3 1.3 collective-permute-start.1
  121.6 4.8 %collective-permute-start = (bf16[2,512,640]{2,1,0:T(8,128)(2,1)S(1)}, bf16[2,512,640]{2,1,0:T(8,128)(2,1)S(1)}, u32[]{:S(2)}, u32[]{:S(2)}) collective-permute-start(bf16[2,512,640]{2,1,0:T(8,128)(2,1)S(1)} %pad_maximum_fusion.1), channel_id=1, source_target_pairs={{0,8},{8,16},{16,24},{24,32},{32,40},{40,48},{48,56},{56,64},{64,7... | collective-permute-start | bytes 3932168 | tf_op jit(solution)/shard_map/ppermute | solution.py:19
  126.5 4.2 %convolution_convert_fusion.2 = bf16[512,640]{1,0:T(8,128)(2,1)S(1)} fusion(bf16[512,5120]{1,0:T(8,128)(2,1)S(1)} %copy-done.4, bf16[5120,640]{1,0:T(8,128)(2,1)S(1)} %bitcast.34), kind=kOutput, calls=%fused_computation.69 | convolution fusion | flops 3355770880 | bytes 12451840 | tf_op jit(solution)/shard_map/dot_general | solution.py:29
  133.3 17.0 %collective-permute-done.1 = bf16[2,512,640]{2,1,0:T(8,128)(2,1)S(1)} collective-permute-done((bf16[2,512,640]{2,1,0:T(8,128)(2,1)S(1)}, bf16[2,512,640]{2,1,0:T(8,128)(2,1)S(1)}, u32[]{:S(2)}, u32[]{:S(2)}) %collective-permute-start.1) | collective-permute-done | bytes 1310752 | tf_op jit(solution)/shard_map/ppermute | solution.py:20
  150.3 1.2 collective-permute-done
  151.5 4.4 %pad_maximum_fusion = bf16[2,1536,640]{2,1,0:T(8,128)(2,1)S(1)} fusion(bf16[2,512,640]{2,1,0:T(8,128)(2,1)S(1)} %collective-permute-done.1, bf16[1,512,640]{2,1,0:T(8,128)(2,1)S(1)} %fusion.43, bf16[1,512,640]{2,1,0:T(8,128)(2,1)S(1)} %fusion.42, bf16[2,512,640]{2,1,0:T(8,128)(2,1)S(1)} %collective-permute-done), kind=kLoop, calls=%fused_computation.4 | loop fusion | flops 15728640 | bytes 7864320 | tf_op jit(solution)/shard_map/concatenate | solution.py:21
  156.2 1.5 fusion.173
  157.6 1.5 fusion.174
  161.4 1.5 fusion.175
  164.0 1.5 fusion.176
  166.6 1.5 fusion.177
  173.8 0.8 fusion.89
  176.1 1.1 copy.9
  (69 shorter events, 17.4 us)
Async XLA Ops:
  6.5 2.2 %copy-start = (bf16[4,128,640]{2,1,0:T(8,128)(2,1)S(1)}, bf16[4,128,640]{2,1,0:T(8,128)(2,1)}, u32[]{:S(2)}) copy-start(bf16[4,128,640]{2,1,0:T(8,128)(2,1)} %param.17) | copy-start | bytes 1966084
  6.5 98.2 %all-gather.2.cloned.1.call-start = ((), (), s32[]{:S(2)}) async-start(), calls=%async_computation.2 | async-start | bytes 5898240 | tf_op jit(solution)/shard_map/all_gather | solution.py:28
  8.7 2.4 %copy-start.2 = (bf16[4,128,640]{2,1,0:T(8,128)(2,1)S(1)}, bf16[4,128,640]{2,1,0:T(8,128)(2,1)}, u32[]{:S(2)}) copy-start(bf16[4,128,640]{2,1,0:T(8,128)(2,1)} %param.16) | copy-start | bytes 1966084
  60.5 3.9 %copy-start.3 = (s32[16,8]{0,1:T(8,128)S(1)}, s32[16,8]{0,1:T(8,128)}, u32[]{:S(2)}) copy-start(s32[16,8]{0,1:T(8,128)} %param.19) | copy-start | bytes 1540
  60.5 4.1 %copy-start.5 = (s32[4]{0:T(128)S(1)}, s32[4]{0:T(128)}, u32[]{:S(2)}) copy-start(s32[4]{0:T(128)} %param.18) | copy-start | bytes 52
  60.5 40.4 %all-to-all-start = ((bf16[16,128,640]{2,1,0:T(8,128)(2,1)}), bf16[16,128,640]{2,1,0:T(8,128)(2,1)S(1)}, u32[]{:S(2)}, u32[]{:S(2)}) async-start(bf16[16,128,640]{2,1,0:T(8,128)(2,1)} %get-tuple-element.14), calls=%async_computation | async-start | bytes 5242880 | tf_op jit(solution)/shard_map/all_to_all | solution.py:54
  104.8 8.8 %copy-start.4 = (bf16[512,5120]{1,0:T(8,128)(2,1)S(1)}, bf16[512,5120]{1,0:T(8,128)(2,1)}, u32[]{:S(2)}) copy-start(bf16[512,5120]{1,0:T(8,128)(2,1)} %all-gather.2.cloned.1.call-done) | copy-start | bytes 15728644
  104.8 21.7 %slice-start = ((s8[6553600]{0:T(1024)(128)(4,1)}), s8[4194304]{0:T(1024)(128)(4,1)S(1)}, s32[]{:S(2)}) async-start(s8[6553600]{0:T(1024)(128)(4,1)} %bitcast.33), calls=%async_computation.3 | async-start | bytes 8388608
  113.6 12.9 %slice-start.1 = ((s8[6553600]{0:T(1024)(128)(4,1)}), s8[2359296]{0:T(1024)(128)(4,1)S(1)}, s32[]{:S(2)}) async-start(s8[6553600]{0:T(1024)(128)(4,1)} %bitcast.33), calls=%async_computation.4 | async-start | bytes 4718592
  120.3 29.9 %collective-permute-start.1 = (bf16[2,512,640]{2,1,0:T(8,128)(2,1)S(1)}, bf16[2,512,640]{2,1,0:T(8,128)(2,1)S(1)}, u32[]{:S(2)}, u32[]{:S(2)}) collective-permute-start(bf16[2,512,640]{2,1,0:T(8,128)(2,1)S(1)} %pad_maximum_fusion.1), channel_id=1, source_target_pairs={{8,0},{16,8},{24,16},{32,24},{40,32},{48,40},{56,48},{64,56},{72,6... | collective-permute-start | bytes 3932168 | tf_op jit(solution)/shard_map/ppermute | solution.py:20
  121.6 29.8 %collective-permute-start = (bf16[2,512,640]{2,1,0:T(8,128)(2,1)S(1)}, bf16[2,512,640]{2,1,0:T(8,128)(2,1)S(1)}, u32[]{:S(2)}, u32[]{:S(2)}) collective-permute-start(bf16[2,512,640]{2,1,0:T(8,128)(2,1)S(1)} %pad_maximum_fusion.1), channel_id=1, source_target_pairs={{0,8},{8,16},{16,24},{24,32},{32,40},{40,48},{48,56},{56,64},{64,7... | collective-permute-start | bytes 3932168 | tf_op jit(solution)/shard_map/ppermute | solution.py:19
  174.6 2.6 %copy-start.1 = (bf16[4,128,640]{2,1,0:T(8,128)(2,1)S(1)}, bf16[4,128,640]{2,1,0:T(8,128)(2,1)}, u32[]{:S(2)}) copy-start(bf16[4,128,640]{2,1,0:T(8,128)(2,1)} %param.17) | copy-start | bytes 1966084
Sparse Core Ops, SparseCore 0:
  9.1 38.8 all-gather.1
where the time goes:
time: 185 us; the launch traced here: 184 us
  waiting for transfers between devices  51.5 us (28%)
  blocking collectives  42 us (23%)
  matrix products  36.3 us (20%)
  other arithmetic  18.7 us (10%)
  between operations  13.8 us (7%)
  local copies, waits for them, and re-layouts  11.8 us (6%)
  starting transfers between devices  9.97 us (5%)
    all_to_all x1, blocking collectives, body(): lax.all_to_all(send_values, 'sp', split_axis=0, concat_axis=0, tiled=True)  42 us
    all_to_all x1, waiting for transfers between devices, body(): lax.all_to_all(send_keys, 'sp', split_axis=0, concat_axis=0, tiled=True)  32.6 us
    ppermute x1, waiting for transfers between devices, with_halo(): after = lax.ppermute(first, axis, down)  17 us
    dot_general x1, matrix products, body(): jnp.dot(gathered, w_value, preferred_element_type=jnp.float32)  8.78 us
    dot_general x5, matrix products, body(): lax.dot_general(query_head, band_keys[:, low:low + HD], contract, preferr...  7.29 us
    dot_general x1, matrix products, body(): jnp.dot(gathered, w_key, preferred_element_type=jnp.float32)  6.58 us
    reduce_sum x10, other arithmetic, body(): total = jnp.sum(band_weights, axis=1) + jnp.sum(cache_weights, axis=1)  5.63 us
    select_n x1, other arithmetic, body(): jnp.where(wanted[:, None, None], jnp.take(cache_values, local_pick, axis=...  4.91 us
  transfers between devices with their start and end apart: 4, of which 3 were waited for; matrix products, arithmetic and copies ran while one was open for 14% of the time, Pallas kernels for 0%

commit v1 on v0

v1 whole, which is shorter than its diff:
```python
import functools
import math

import jax
import jax.numpy as jnp
from jax import lax
from jax.experimental import pallas as pl
from jax.experimental.pallas import tpu as pltpu
from jax.sharding import PartitionSpec as P

HD = 128
TILE = 128
BLOCK = 128
MESH = pl.DeviceIdType.MESH
LOW = -1e30
SCALE = math.log2(math.e) / math.sqrt(HD)
ROUNDS = ((0, 1), (1, 2), (3, 1))
COLUMN = (0, 1, 3, 2)


def kernel(
    tokens, w_query, w_key, w_value, cache_keys, cache_values, tile_level, window_map,
    out,
    tok, weights, total, q_buf, kv_own, halo, held_0, held_1, held_2, held_3, send, row, passing, m_buf, l_buf, acc_buf,
    weight_sem, local_sem, send_sem, recv_sem,
):
    sp = lax.axis_index("sp")
    tp = lax.axis_index("tp")
    z, y = sp // 4, sp % 4
    x, core = tp // 2, tp % 2
    rows, width = tokens.shape
    heads = width // HD

    sibling = (sp, x * 2 + 1 - core)
    x_up = (sp, ((x + 1) % 4) * 2 + core)
    x_down = (sp, ((x + 3) % 4) * 2 + core)
    y_up = (z * 4 + (y + 1) % 4, tp)
    y_down = (z * 4 + (y + 3) % 4, tp)
    z_up = (((z + 1) % 4) * 4 + y, tp)
    z_down = (((z + 3) % 4) * 4 + y, tp)
    after = ((sp + 1) % 16, tp)
    before = ((sp + 15) % 16, tp)
    gathered = (held_0, held_1, held_2, held_3)
    peers = (sibling, x_up, x_down, y_up, y_down, z_up, z_down, after, before)

    barrier = pltpu.get_barrier_semaphore()
    for peer in peers:
        pl.semaphore_signal(barrier, inc=1, device_id=peer, device_id_type=MESH)

    lane = pl.ds(pl.multiple_of(core * width, HD), width)
    own_tokens = pltpu.make_async_copy(tokens, tok.at[0, :, lane], local_sem.at[0])
    own_keys = pltpu.make_async_copy(cache_keys, gathered[0].at[0], local_sem.at[1])
    own_values = pltpu.make_async_copy(cache_values, gathered[0].at[1], local_sem.at[2])
    own_keys.start()
    own_values.start()
    own_tokens.start()
    depth = 2 * width
    weight_copies = {}
    for back in (0, 1, 3, 2):
        source = pl.ds(pl.multiple_of(((x + 4 - back) % 4) * depth, depth), depth)
        for j, w in enumerate((w_query, w_key, w_value)):
            copy = pltpu.make_async_copy(
                w.at[source, :], weights.at[back, :, pl.ds(j * width, width)], weight_sem.at[back, j]
            )
            copy.start()
            weight_copies[back, j] = copy

    pl.semaphore_wait(barrier, len(peers))

    copies = []

    def remote(src, dst, peer):
        at = len(copies)
        copy = pltpu.make_async_remote_copy(
            src_ref=src, dst_ref=dst, send_sem=send_sem.at[at], recv_sem=recv_sem.at[at],
            device_id=peer, device_id_type=MESH,
        )
        copy.start()
        copies.append(copy)
        return copy

    to_sibling = [remote(tokens, tok.at[0, :, lane], sibling)]
    y_first = []
    for kv, cache in enumerate((cache_keys, cache_values)):
        y_first.append(remote(cache, gathered[1].at[kv], y_up))
        y_first.append(remote(cache, gathered[3].at[kv], y_down))
    x_from_down = remote(tokens, tok.at[1, :, lane], x_up)
    x_from_up = remote(tokens, tok.at[3, :, lane], x_down)

    def wanted(holder, owner):
        local, found = jnp.int32(0), jnp.int32(0)
        for k in range(8):
            block = window_map[owner, k]
            hit = jnp.where(block // 4 == holder, 1, 0)
            local = local + hit * (block % 4)
            found = found + hit
        return local, found

    def pick(position):
        column = COLUMN[position]
        holder = z * 4 + (y + 4 - column) % 4
        for step, owner_z in ((0, z), (1, (z + 1) % 4), (2, (z + 2) % 4), (3, (z + 3) % 4)):
            local, _ = wanted(holder, owner_z * 4 + y)
            for kv in range(2):
                block = gathered[column][kv, local]
                if step == 0:
                    row[kv, 0, position] = block
                else:
                    send[kv, step - 1, position] = block

    z_copies = {}

    def z_send(number):
        first, count = ROUNDS[number]
        slots = pl.ds(first, count)
        far_keys = remote(send.at[0, 1, slots], passing.at[0, slots], z_up)
        far_values = remote(send.at[1, 1, slots], passing.at[1, slots], z_down)
        near = []
        for kv in range(2):
            near.append(remote(send.at[kv, 0, slots], row.at[kv, 1, slots], z_up))
            near.append(remote(send.at[kv, 2, slots], row.at[kv, 3, slots], z_down))
        z_copies[number] = (far_keys, far_values, near)

    z_far = {}

    def z_pass(number):
        first, count = ROUNDS[number]
        slots = pl.ds(first, count)
        far_keys, far_values, _ = z_copies[number]
        far_keys.wait_recv()
        a = remote(passing.at[0, slots], row.at[0, 2, slots], z_up)
        far_values.wait_recv()
        b = remote(passing.at[1, slots], row.at[1, 2, slots], z_down)
        z_far[number] = (a, b)

    def project(back, start):
        for j in range(3):
            weight_copies[back, j].wait()

        @pl.loop(0, 3)
        def _(j):
            columns = pl.ds(pl.multiple_of(j * width, HD), width)
            product = jnp.dot(tok[back], weights[back, :, columns], preferred_element_type=jnp.float32)
            if start:
                total[:, columns] = product
            else:
                total[:, columns] += product

    own_keys.wait()
    own_values.wait()
    pick(0)
    z_send(0)

    own_tokens.wait()
    to_sibling[0].wait_recv()
    project(0, True)
    z_pass(0)

    half = rows // 2
    x_from_down.wait_recv()
    x_far = [remote(tok.at[1, pl.ds(0, half), lane], tok.at[2, pl.ds(0, half), lane], x_up)]
    x_from_up.wait_recv()
    x_far.append(remote(tok.at[3, pl.ds(half, half), lane], tok.at[2, pl.ds(half, half), lane], x_down))
    sibling_down = remote(tok.at[1, :, lane], tok.at[1, :, lane], sibling)
    sibling_up = remote(tok.at[3, :, lane], tok.at[3, :, lane], sibling)
    sibling_down.wait_recv()
    project(1, False)
    sibling_up.wait_recv()
    project(3, False)
    sibling_far = []
    for part in range(2):
        piece = pl.ds(part * half, half)
        x_far[part].wait_recv()
        sibling_far.append(remote(tok.at[2, piece, lane], tok.at[2, piece, lane], sibling))
    for copy in sibling_far:
        copy.wait_recv()
    project(2, False)

    @pl.loop(0, heads)
    def _(h):
        q_buf[h] = total[:, pl.ds(pl.multiple_of(h * HD, HD), HD)].astype(jnp.bfloat16)

    kv_own[0] = total[:, width : 2 * width].astype(jnp.bfloat16)
    kv_own[1] = total[:, 2 * width : 3 * width].astype(jnp.bfloat16)

    for copy in y_first:
        copy.wait_recv()
    y_far = []
    for kv in range(2):
        low, high = pl.ds(0, 2), pl.ds(2, 2)
        y_far.append(remote(gathered[1].at[kv, low], gathered[2].at[kv, low], y_up))
        y_far.append(remote(gathered[3].at[kv, high], gathered[2].at[kv, high], y_down))
    pick(1)
    pick(2)
    z_send(1)
    halo_copies = []
    for kv in range(2):
        halo_copies.append(remote(kv_own.at[kv], halo.at[0, kv], after))
        halo_copies.append(remote(kv_own.at[kv], halo.at[1, kv], before))

    part_rows = rows // 2

    def attend(keys_of, values_of, adjust, count, first=False):
        @pl.loop(0, 2 * heads)
        def _(step):
            h = step // 2
            part = step % 2
            lanes = pl.ds(pl.multiple_of(h * HD, HD), HD)
            at = pl.ds(pl.multiple_of(part * part_rows, part_rows), part_rows)
            q = q_buf[h, at]
            scores = lax.dot_general(
                q, keys_of(lanes), (((1,), (1,)), ((), ())), preferred_element_type=jnp.float32
            )
            pieces = [
                adjust(i, scores[:, i * BLOCK : (i + 1) * BLOCK] * SCALE, part) for i in range(count)
            ]
            top = functools.reduce(jnp.maximum, pieces)
            top = jnp.broadcast_to(jnp.max(top, axis=1, keepdims=True), (part_rows, HD))
            if not first:
                old = m_buf[h, at]
                top = jnp.maximum(top, old)
                keep = jnp.exp2(old - top)
            pieces = [jnp.exp2(piece - top) for piece in pieces]
            total_new = functools.reduce(jnp.add, pieces)
            mixed = jnp.dot(
                jnp.concatenate([piece.astype(jnp.bfloat16) for piece in pieces], axis=1),
                values_of(lanes),
                preferred_element_type=jnp.float32,
            )
            m_buf[h, at] = top
            if first:
                l_buf[h, at] = total_new
                acc_buf[h, at] = mixed
            else:
                l_buf[h, at] = l_buf[h, at] * keep + total_new
                acc_buf[h, at] = acc_buf[h, at] * keep + mixed

    row_at = lax.broadcasted_iota(jnp.int32, (part_rows, BLOCK), 0)
    column_at = lax.broadcasted_iota(jnp.int32, (part_rows, BLOCK), 1)

    def radius_of(part):
        low = (tile_level[part * 2] + 1) * rows // 3
        high = (tile_level[part * 2 + 1] + 1) * rows // 3
        return jnp.where(row_at < TILE, low, high)

    def band(offset, exists):
        def adjust(i, piece, part):
            distance = jnp.abs(column_at - row_at + (i * BLOCK + offset - part * part_rows))
            radius = radius_of(part)
            if exists is not None:
                radius = jnp.where(exists, radius, -1)
            return jnp.where(distance <= radius, piece, LOW)

        return adjust

    def slots(places):
        bias = []
        for back, position in places:
            holder = ((z + 4 - back) % 4) * 4 + (y + 4 - COLUMN[position]) % 4
            _, found = wanted(holder, sp)
            bias.append(jnp.where(found > 0, 0.0, LOW).astype(jnp.float32))

        def side(kv):
            return lambda lanes: jnp.concatenate([row[kv, b, p, :, lanes] for b, p in places], axis=0)

        attend(side(0), side(1), lambda i, piece, part: piece + bias[i], len(places))

    def rows_of(ref):
        return lambda lanes: ref[:, lanes]

    attend(rows_of(kv_own.at[0]), rows_of(kv_own.at[1]), band(0, None), 4, first=True)

    for copy in z_copies[0][2] + list(z_far[0]):
        copy.wait_recv()
    slots(((0, 0), (0, 1), (0, 2), (1, 0), (2, 0), (3, 0)))

    z_pass(1)
    for copy in y_far:
        copy.wait_recv()
    pick(3)
    z_send(2)
    for copy in z_copies[1][2]:
        copy.wait_recv()
    slots(((1, 1), (1, 2), (3, 1), (3, 2)))
    z_pass(2)
    for copy in z_far[1]:
        copy.wait_recv()
    slots(((2, 1), (2, 2)))
    for copy in halo_copies:
        copy.wait_recv()
    attend(rows_of(halo.at[0, 0]), rows_of(halo.at[0, 1]), band(-rows, sp > 0), 4)
    attend(rows_of(halo.at[1, 0]), rows_of(halo.at[1, 1]), band(rows, sp < 15), 4)
    for copy in z_copies[2][2] + list(z_far[2]):
        copy.wait_recv()
    slots(((0, 3), (1, 3), (2, 3), (3, 3)))

    @pl.loop(0, heads)
    def _(h):
        lanes = pl.ds(pl.multiple_of(h * HD, HD), HD)
        out[:, lanes] = (acc_buf[h] / jnp.sum(l_buf[h], axis=1, keepdims=True)).astype(out.dtype)

    for copy in copies:
        copy.wait_send()


def body(tokens, w_query, w_key, w_value, cache_keys, cache_values, tile_level, window_map):
    rows, width = tokens.shape
    heads = width // HD
    bf16, f32 = jnp.bfloat16, jnp.float32
    block = (BLOCK, width)
    n_copies = 48
    return pl.pallas_call(
        kernel,
        out_shape=jax.ShapeDtypeStruct((rows, width), bf16),
        in_specs=[pl.BlockSpec(memory_space=pl.ANY)] * 6 + [pl.BlockSpec(memory_space=pltpu.SMEM)] * 2,
        out_specs=pl.BlockSpec(memory_space=pltpu.VMEM),
        scratch_shapes=[
            pltpu.VMEM((4, rows, 2 * width), bf16),
            pltpu.VMEM((4, 2 * width, 3 * width), bf16),
            pltpu.VMEM((rows, 3 * width), f32),
            pltpu.VMEM((heads, rows, HD), bf16),
            pltpu.VMEM((2, rows, width), bf16),
            pltpu.VMEM((2, 2, rows, width), bf16),
            pltpu.VMEM((2, 4) + block, bf16),
            pltpu.VMEM((2, 4) + block, bf16),
            pltpu.VMEM((2, 4) + block, bf16),
            pltpu.VMEM((2, 4) + block, bf16),
            pltpu.VMEM((2, 3, 4) + block, bf16),
            pltpu.VMEM((2, 4, 4) + block, bf16),
            pltpu.VMEM((2, 4) + block, bf16),
            pltpu.VMEM((heads, rows, HD), f32),
            pltpu.VMEM((heads, rows, HD), f32),
            pltpu.VMEM((heads, rows, HD), f32),
            pltpu.SemaphoreType.DMA((4, 3)),
            pltpu.SemaphoreType.DMA((3,)),
            pltpu.SemaphoreType.DMA((n_copies,)),
            pltpu.SemaphoreType.DMA((n_copies,)),
        ],
        compiler_params=pltpu.CompilerParams(
            collective_id=0, has_side_effects=True, vmem_limit_bytes=60 * 1024 * 1024
        ),
    )(tokens, w_query, w_key, w_value, cache_keys, cache_values, tile_level, window_map)


def solution(mesh):
    placed = (
        P("sp", "tp"),
        P(None, "tp"),
        P(None, "tp"),
        P(None, "tp"),
        P("sp", None, "tp"),
        P("sp", None, "tp"),
        P("sp"),
        P(),
    )
    return jax.shard_map(body, mesh=mesh, in_specs=placed, out_specs=P("sp", "tp"), check_vma=False)
```

time: 185 us -> 127 us (0.69)
  Pallas kernels: 0 us -> 123 us
  waiting for transfers between devices: 51.5 us -> 0 us
  blocking collectives: 42 us -> 0 us
  matrix products: 36.3 us -> 0 us
  other arithmetic: 18.7 us -> 0 us
  between operations: 13.8 us -> 0.01 us
  starting transfers between devices: 9.97 us -> 0 us
  local copies, waits for them, and re-layouts: 11.8 us -> 3.33 us
    pallas_call x0 -> x1, Pallas kernels: none -> 123 us  [body(): pl.pallas_call(kernel, out_shape=jax.ShapeDtypeStruct((rows, width), bf16...]
    all_to_all x1 -> x0, blocking collectives: 42 us -> none  [body(): lax.all_to_all(send_values, 'sp', split_axis=0, concat_axis=0, tiled=True)]
    dot_general x23 -> x0, matrix products: 36.3 us -> none  [the longest x1 8.78 us: body(): jnp.dot(gathered, w_value, preferred_element_type=jnp.float32)]
    all_to_all x1 -> x0, waiting for transfers between devices: 32.6 us -> none  [body(): lax.all_to_all(send_keys, 'sp', split_axis=0, concat_axis=0, tiled=True)]
    ppermute x2 -> x0, waiting for transfers between devices: 18.1 us -> none  [the longest x1 17 us: with_halo(): after = lax.ppermute(first, axis, down)]
    gather x4 -> x0, local copies, waits for them, and re-layouts: 10.1 us -> none  [the longest x1 3.52 us: body(): jnp.take(received_values, own_holders, axis=0).reshape(-1, local_width)]
    select_n x4 -> x0, other arithmetic: 7.05 us -> none  [the longest x1 4.91 us: body(): jnp.where(wanted[:, None, None], jnp.take(cache_values, local_pick, axis=...]
    reduce_sum x11 -> x0, other arithmetic: 6.34 us -> none  [the longest x10 5.63 us: body(): total = jnp.sum(band_weights, axis=1) + jnp.sum(cache_weights, axis=1)]
  transfers between devices with their start and end apart: 4 -> 0, of which waited for: 3 -> 0; matrix products, arithmetic and copies ran while one was open for 14% -> 0% of each run, Pallas kernels for 0% -> 0%
where the time goes in v1:
time: 127 us
  Pallas kernels  123 us (97%)
  local copies, waits for them, and re-layouts  3.33 us (3%)
    pallas_call x1, Pallas kernels, body(): pl.pallas_call(kernel, out_shape=jax.ShapeDtypeStruct((rows, width), bf16...  123 us
    unnamed x2, local copies, waits for them, and re-layouts  3.33 us

profile of v1, /device:TPU:0, one launch (start us, length us, event | category | flops | bytes accessed | tf_op | source)
XLA Modules:
  0.0 126.8 jit_solution(3938529306928626095)
XLA Ops:
  0.0 1.4 %copy.9.window_map = s32[16,8]{1,0:T(8,128)} copy(s32[16,8]{0,1:T(8,128)} %param.15) | data formatting | bytes 1024 | tf_op args[7]
  1.4 123.4 %shard_map.82 = bf16[512,640]{1,0:T(8,128)(2,1)} custom-call(bf16[512,640]{1,0:T(8,128)(2,1)} %tokens.1, bf16[5120,640]{1,0:T(8,128)(2,1)} %w_query.1, bf16[5120,640]{1,0:T(8,128)(2,1)} %w_key.1, bf16[5120,640]{1,0:T(8,128)(2,1)} %w_value.1, bf16[4,128,640]{2,1,0:T(8,128)(2,1)} %cache_keys.1, bf16[4,128,640]{2,1,0:T(8,128)(2,1)} %cache_values.1, ...), custom_call_target="tpu_custom_call" | custom-call | tf_op jit(solution)/shard_map/pallas_call | solution.py:312
  124.8 2.0 %copy.11 = bf16[512,640]{1,0:T(8,128)(2,1)} copy(bf16[512,640]{1,0:T(8,128)(2,1)} %shard_map.82) | data formatting | bytes 1310720

commit v2 on v1

v2 whole, which is shorter than its diff:
```python
import functools
import math

import jax
import jax.numpy as jnp
from jax import lax
from jax.experimental import pallas as pl
from jax.experimental.pallas import tpu as pltpu
from jax.sharding import PartitionSpec as P

HD = 128
TILE = 128
BLOCK = 128
MESH = pl.DeviceIdType.MESH
LOW = -1e30
SCALE = math.log2(math.e) / math.sqrt(HD)
COLUMN = (0, 1, 3, 2)
N_COPIES = 64


def kernel(
    tokens, w_query, w_key, w_value, cache_keys, cache_values, tile_level, window_map,
    out,
    tok, weights, total, q_buf, kv_own, halo, k_0, k_1, k_2, k_3, v_0, v_1, v_2, v_3, send, row,
    m_buf, acc_buf, bias_own, bias_halo, turning,
    weight_sem, local_sem, send_sem, recv_sem,
):
    sp = lax.axis_index("sp")
    tp = lax.axis_index("tp")
    z, y = sp // 4, sp % 4
    x, core = tp // 2, tp % 2
    rows, width = tokens.shape
    heads = width // HD
    half = rows // 2
    f32, bf16 = jnp.float32, jnp.bfloat16

    sibling = (sp, x * 2 + 1 - core)
    x_up = (sp, ((x + 1) % 4) * 2 + core)
    x_down = (sp, ((x + 3) % 4) * 2 + core)
    y_up = (z * 4 + (y + 1) % 4, tp)
    y_down = (z * 4 + (y + 3) % 4, tp)
    z_up = (((z + 1) % 4) * 4 + y, tp)
    z_down = (((z + 3) % 4) * 4 + y, tp)
    z_far = (((z + 2) % 4) * 4 + y, tp)
    after = ((sp + 1) % 16, tp)
    before = ((sp + 15) % 16, tp)
    held = ((k_0, v_0), (k_1, v_1), (k_2, v_2), (k_3, v_3))
    peers = (sibling, x_up, x_down, y_up, y_down, z_up, z_down, z_far, after, before)

    barrier = pltpu.get_barrier_semaphore()
    for peer in peers:
        pl.semaphore_signal(barrier, inc=1, device_id=peer, device_id_type=MESH)

    lane = pl.ds(pl.multiple_of(core * width, HD), width)
    own_tokens = pltpu.make_async_copy(tokens, tok.at[0, :, lane], local_sem.at[0])
    own_blocks = [
        pltpu.make_async_copy(cache, held[0][kv], local_sem.at[1 + kv])
        for kv, cache in enumerate((cache_keys, cache_values))
    ]
    own_blocks[0].start()
    own_blocks[1].start()
    own_tokens.start()
    depth = 2 * width
    weight_copies = {}
    for back in (0, 1, 3, 2):
        source = pl.ds(pl.multiple_of(((x + 4 - back) % 4) * depth, depth), depth)
        for j, w in enumerate((w_query, w_key, w_value)):
            copy = pltpu.make_async_copy(
                w.at[source, :], weights.at[back, :, pl.ds(j * width, width)], weight_sem.at[back, j]
            )
            copy.start()
            weight_copies[back, j] = copy

    pl.semaphore_wait(barrier, len(peers))

    copies = []

    def remote(src, dst, peer):
        at = len(copies)
        copy = pltpu.make_async_remote_copy(
            src_ref=src, dst_ref=dst, send_sem=send_sem.at[at], recv_sem=recv_sem.at[at],
            device_id=peer, device_id_type=MESH,
        )
        copy.start()
        copies.append(copy)
        return copy

    y_near = {0: [remote(cache_keys, held[1][0], y_up), remote(cache_keys, held[3][0], y_down)]}
    x_from_down = remote(tokens, tok.at[1, :, lane], x_up)
    x_from_up = remote(tokens, tok.at[3, :, lane], x_down)
    from_sibling = remote(tokens, tok.at[0, :, lane], sibling)
    y_near[1] = [remote(cache_values, held[1][1], y_up), remote(cache_values, held[3][1], y_down)]

    def wanted(holder, owner):
        local, found = jnp.int32(0), jnp.int32(0)
        for k in range(8):
            block = window_map[owner, k]
            hit = jnp.where(block // 4 == holder, 1, 0)
            local = local + hit * (block % 4)
            found = found + hit
        return local, found

    z_copies = {}

    def z_send(kv, first, count):
        for position in range(first, first + count):
            column = COLUMN[position]
            holder = z * 4 + (y + 4 - column) % 4
            for step in range(4):
                local, _ = wanted(holder, ((z + step) % 4) * 4 + y)
                block = held[column][kv][local]
                if step == 0:
                    row[kv, 0, position] = block
                else:
                    send[kv, step - 1, position] = block
        slots = pl.ds(first, count)
        z_copies[kv, first] = [
            remote(send.at[kv, 1, slots], row.at[kv, 2, slots], z_far),
            remote(send.at[kv, 0, slots], row.at[kv, 1, slots], z_up),
            remote(send.at[kv, 2, slots], row.at[kv, 3, slots], z_down),
        ]

    y_far = {}

    def y_pass(kv):
        low, high = pl.ds(0, 2), pl.ds(2, 2)
        for copy in y_near[kv]:
            copy.wait_recv()
        y_far[kv] = [
            remote(held[1][kv].at[low], held[2][kv].at[low], y_up),
            remote(held[3][kv].at[high], held[2][kv].at[high], y_down),
        ]

    def project(back, start):
        for j in range(3):
            weight_copies[back, j].wait()

        @pl.loop(0, 3)
        def _(j):
            columns = pl.ds(pl.multiple_of(j * width, HD), width)
            product = jnp.dot(tok[back], weights[back, :, columns], preferred_element_type=f32)
            if start:
                total[:, columns] = product
            else:
                total[:, columns] += product

    for kv in range(2):
        own_blocks[kv].wait()
        z_send(kv, 0, 1)

    own_tokens.wait()
    from_sibling.wait_recv()
    project(0, True)

    def radius_of(first, count):
        at = lax.broadcasted_iota(jnp.int32, (count, 1), 0) + first
        radius = jnp.zeros((count, 1), jnp.int32)
        for tile in range(rows // TILE):
            radius = jnp.where(at // TILE == tile, (tile_level[tile] + 1) * rows // 3, radius)
        return radius, at

    def bias_of(first, count, key_first, key_count, exists):
        radius, at = radius_of(first, count)
        key_at = lax.broadcasted_iota(jnp.int32, (count, key_count), 1) + key_first
        allowed = jnp.abs(key_at - at) <= radius
        if exists is not None:
            allowed = allowed & exists
        return jnp.where(allowed, 0.0, LOW).astype(f32)

    for part in range(2):
        first = part * half
        bias_own[pl.ds(first, half), :] = bias_of(first, half, 0, rows, None)
        left = rows - first
        bias_halo[part, :, pl.ds(0, left)] = bias_of(first, half, first - rows, left, sp > 0)
        bias_halo[part, :, pl.ds(left, half + first)] = bias_of(first, half, rows, half + first, sp < 15)

    y_pass(0)
    z_send(0, 1, 2)

    x_from_down.wait_recv()
    x_far = [remote(tok.at[1, pl.ds(0, half), lane], tok.at[2, pl.ds(0, half), lane], x_up)]
    x_from_up.wait_recv()
    x_far.append(remote(tok.at[3, pl.ds(half, half), lane], tok.at[2, pl.ds(half, half), lane], x_down))
    sibling_down = remote(tok.at[1, :, lane], tok.at[1, :, lane], sibling)
    sibling_up = remote(tok.at[3, :, lane], tok.at[3, :, lane], sibling)
    sibling_down.wait_recv()
    project(1, False)
    sibling_up.wait_recv()
    project(3, False)
    sibling_far = []
    for part in range(2):
        piece = pl.ds(part * half, half)
        x_far[part].wait_recv()
        sibling_far.append(remote(tok.at[2, piece, lane], tok.at[2, piece, lane], sibling))
    for copy in sibling_far:
        copy.wait_recv()
    project(2, False)

    for h in range(heads):
        for j in range(3):
            part = total[:, pl.ds(j * width + h * HD, HD)].astype(bf16)
            if j == 0:
                q_buf[h] = part
            else:
                kv_own[j - 1, h] = part

    y_pass(1)
    z_send(1, 1, 2)
    halo_copies = {}
    turns = []

    def describe(src, dst, send_at, recv_at, peer):
        return pltpu.make_async_remote_copy(
            src_ref=src, dst_ref=dst, send_sem=send_sem.at[send_at], recv_sem=recv_sem.at[recv_at],
            device_id=peer, device_id_type=MESH,
        )

    for h in range(heads):
        halo_copies[h] = []
        for side, peer in ((0, after), (1, before)):
            halo_copies[h].append(remote(kv_own.at[0, h], halo.at[side, 0, h], peer))
        turn_at = N_COPIES - 1 - h
        for side, peer, last, z_next, y_next in ((0, after, 3, z_up, y_up), (1, before, 0, z_down, y_down)):
            at = len(copies)
            source, place = kv_own.at[1, h], halo.at[side, 1, h]
            straight = describe(source, place, at, at, peer)
            turn = describe(source, turning.at[h], at, turn_at, z_next)
            onward = describe(turning.at[h], place, turn_at, at, y_next)
            copies.append(straight)
            halo_copies[h].append(straight)
            turns.append((last, turn, onward))

            @pl.when(y != last)
            def _():
                straight.start()

            @pl.when(y == last)
            def _():
                turn.start()

    def turn_values():
        for last, turn, onward in turns:

            @pl.when(y == last)
            def _():
                turn.wait_recv()
                onward.start()

    ones = jnp.ones((BLOCK, HD), bf16)

    def attend(h, at, scores, values, count, first=False):
        pieces = [scores[:, i * BLOCK : (i + 1) * BLOCK] for i in range(count)]
        top = functools.reduce(jnp.maximum, pieces)
        top = jnp.broadcast_to(jnp.max(top, axis=1, keepdims=True), pieces[0].shape)
        if not first:
            old = m_buf[h, at]
            top = jnp.maximum(top, old)
            keep = jnp.exp2((old - top) * SCALE)
        scaled = top * SCALE
        weight = jnp.concatenate(
            [jnp.exp2(piece * SCALE - scaled).astype(bf16) for piece in pieces], axis=1
        )
        values = jnp.concatenate([values, jnp.concatenate([ones] * count, axis=0)], axis=1)
        mixed = jnp.dot(weight, values, preferred_element_type=f32)
        m_buf[h, at] = top
        for side in range(2):
            lanes = pl.ds(side * HD, HD)
            part = mixed[:, side * HD : (side + 1) * HD]
            acc_buf[h, at, lanes] = part if first else acc_buf[h, at, lanes] * keep + part

    contract = (((1,), (1,)), ((), ()))

    def slots(places):
        everything = pl.ds(0, rows)
        count = len(places)
        first_lane = lax.broadcasted_iota(jnp.int32, (BLOCK, HD), 1) == 0
        bias = []
        for back, position in places:
            holder = ((z + 4 - back) % 4) * 4 + (y + 4 - COLUMN[position]) % 4
            _, found = wanted(holder, sp)
            low = jnp.where(found > 0, 0.0, LOW).astype(f32)
            bias.append(jnp.where(first_lane, low, 0.0).astype(bf16))
        bias = jnp.concatenate(bias, axis=0)
        pointer = jnp.where(lax.broadcasted_iota(jnp.int32, (rows, HD), 1) == 0, 1.0, 0.0).astype(bf16)
        for h in range(heads):
            lanes = pl.ds(h * HD, HD)
            keys = jnp.concatenate([row[0, b, p, :, lanes] for b, p in places], axis=0)
            values = jnp.concatenate([row[1, b, p, :, lanes] for b, p in places], axis=0)
            scores = lax.dot_general(
                jnp.concatenate([q_buf[h], pointer], axis=1),
                jnp.concatenate([keys, bias], axis=1),
                contract,
                preferred_element_type=f32,
            )
            attend(h, everything, scores, values, count)

    for h in range(heads):
        scores = lax.dot_general(q_buf[h], kv_own[0, h], contract, preferred_element_type=f32)
        attend(h, pl.ds(0, rows), scores + bias_own[...], kv_own[1, h], 4, first=True)

    for copy in y_far[0]:
        copy.wait_recv()
    z_send(0, 3, 1)
    for copy in z_copies[0, 0] + z_copies[1, 0]:
        copy.wait_recv()
    slots(((0, 0), (0, 1), (0, 2), (1, 0), (2, 0), (3, 0)))
    for copy in y_far[1]:
        copy.wait_recv()
    z_send(1, 3, 1)
    for copy in z_copies[0, 1] + z_copies[1, 1]:
        copy.wait_recv()
    slots(((1, 1), (1, 2), (2, 1), (2, 2), (3, 1), (3, 2)))
    turn_values()
    for copy in z_copies[0, 3] + z_copies[1, 3]:
        copy.wait_recv()
    slots(((0, 3), (1, 3), (2, 3), (3, 3)))

    for h in range(heads):
        for copy in halo_copies[h]:
            copy.wait_recv()
        for part in range(2):
            at = pl.ds(part * half, half)
            left = pl.ds(part * half, rows - part * half)
            right = pl.ds(0, half + part * half)
            keys = jnp.concatenate([halo[0, 0, h, left], halo[1, 0, h, right]], axis=0)
            values = jnp.concatenate([halo[0, 1, h, left], halo[1, 1, h, right]], axis=0)
            scores = lax.dot_general(q_buf[h, at], keys, contract, preferred_element_type=f32)
            attend(h, at, scores + bias_halo[part], values, 6)
        sums = acc_buf[h]
        out[:, pl.ds(h * HD, HD)] = (sums[:, :HD] / sums[:, HD:]).astype(out.dtype)

    for copy in copies:
        copy.wait_send()
    for last, _, onward in turns:

        @pl.when(y == last)
        def _():
            onward.wait_send()


def body(tokens, w_query, w_key, w_value, cache_keys, cache_values, tile_level, window_map):
    rows, width = tokens.shape
    heads = width // HD
    bf16, f32 = jnp.bfloat16, jnp.float32
    block = (BLOCK, width)
    return pl.pallas_call(
        kernel,
        out_shape=jax.ShapeDtypeStruct((rows, width), bf16),
        in_specs=[pl.BlockSpec(memory_space=pl.ANY)] * 6 + [pl.BlockSpec(memory_space=pltpu.SMEM)] * 2,
        out_specs=pl.BlockSpec(memory_space=pltpu.VMEM),
        scratch_shapes=[
            pltpu.VMEM((4, rows, 2 * width), bf16),
            pltpu.VMEM((4, 2 * width, 3 * width), bf16),
            pltpu.VMEM((rows, 3 * width), f32),
            pltpu.VMEM((heads, rows, HD), bf16),
            pltpu.VMEM((2, heads, rows, HD), bf16),
            pltpu.VMEM((2, 2, heads, rows, HD), bf16),
            pltpu.VMEM((4,) + block, bf16),
            pltpu.VMEM((4,) + block, bf16),
            pltpu.VMEM((4,) + block, bf16),
            pltpu.VMEM((4,) + block, bf16),
            pltpu.VMEM((4,) + block, bf16),
            pltpu.VMEM((4,) + block, bf16),
            pltpu.VMEM((4,) + block, bf16),
            pltpu.VMEM((4,) + block, bf16),
            pltpu.VMEM((2, 3, 4) + block, bf16),
            pltpu.VMEM((2, 4, 4) + block, bf16),
            pltpu.VMEM((heads, rows, HD), f32),
            pltpu.VMEM((heads, rows, 2 * HD), f32),
            pltpu.VMEM((rows, rows), f32),
            pltpu.VMEM((2, rows // 2, 3 * rows // 2), f32),
            pltpu.VMEM((heads, rows, HD), bf16),
            pltpu.SemaphoreType.DMA((4, 3)),
            pltpu.SemaphoreType.DMA((3,)),
            pltpu.SemaphoreType.DMA((N_COPIES,)),
            pltpu.SemaphoreType.DMA((N_COPIES,)),
        ],
        compiler_params=pltpu.CompilerParams(
            collective_id=0, has_side_effects=True, vmem_limit_bytes=62 * 1024 * 1024
        ),
    )(tokens, w_query, w_key, w_value, cache_keys, cache_values, tile_level, window_map)


def solution(mesh):
    placed = (
        P("sp", "tp"),
        P(None, "tp"),
        P(None, "tp"),
        P(None, "tp"),
        P("sp", None, "tp"),
        P("sp", None, "tp"),
        P("sp"),
        P(),
    )
    return jax.shard_map(body, mesh=mesh, in_specs=placed, out_specs=P("sp", "tp"), check_vma=False)
```

time: 127 us -> 97.9 us (0.77)
  Pallas kernels: 123 us -> 93.5 us
    pallas_call x1, Pallas kernels: 123 us -> 93.5 us  [body(): pl.pallas_call(kernel, out_shape=jax.ShapeDtypeStruct((rows, width), bf16...]
where the time goes in v2:
time: 97.9 us; the launch traced here: 96.8 us
  Pallas kernels  93.5 us (96%)
  local copies, waits for them, and re-layouts  3.33 us (3%)
    pallas_call x1, Pallas kernels, body(): pl.pallas_call(kernel, out_shape=jax.ShapeDtypeStruct((rows, width), bf16...  93.5 us
    unnamed x2, local copies, waits for them, and re-layouts  3.33 us

profile of v2, /device:TPU:0, one launch (start us, length us, event | category | flops | bytes accessed | tf_op | source)
XLA Modules:
  0.0 96.8 jit_solution(11691772856931046945)
XLA Ops:
  0.0 1.4 %copy.9.window_map = s32[16,8]{1,0:T(8,128)} copy(s32[16,8]{0,1:T(8,128)} %param.15) | data formatting | bytes 1024 | tf_op args[7]
  1.4 93.5 %shard_map.82 = bf16[512,640]{1,0:T(8,128)(2,1)} custom-call(bf16[512,640]{1,0:T(8,128)(2,1)} %tokens.1, bf16[5120,640]{1,0:T(8,128)(2,1)} %w_query.1, bf16[5120,640]{1,0:T(8,128)(2,1)} %w_key.1, bf16[5120,640]{1,0:T(8,128)(2,1)} %w_value.1, bf16[4,128,640]{2,1,0:T(8,128)(2,1)} %cache_keys.1, bf16[4,128,640]{2,1,0:T(8,128)(2,1)} %cache_values.1, ...), custom_call_target="tpu_custom_call" | custom-call | tf_op jit(solution)/shard_map/pallas_call | solution.py:346
  94.8 2.0 %copy.11 = bf16[512,640]{1,0:T(8,128)(2,1)} copy(bf16[512,640]{1,0:T(8,128)(2,1)} %shard_map.82) | data formatting | bytes 1310720

commit v3 on v2

--- a/solution.py
+++ b/solution.py
@@ -15,15 +15,15 @@
 LOW = -1e30
 SCALE = math.log2(math.e) / math.sqrt(HD)
 COLUMN = (0, 1, 3, 2)
-N_COPIES = 64
+N_COPIES = 96
 
 
 def kernel(
     tokens, w_query, w_key, w_value, cache_keys, cache_values, tile_level, window_map,
     out,
-    tok, weights, total, q_buf, kv_own, halo, k_0, k_1, k_2, k_3, v_0, v_1, v_2, v_3, send, row,
-    m_buf, acc_buf, bias_own, bias_halo, turning,
-    weight_sem, local_sem, send_sem, recv_sem,
+    tok, tok_near, weights, total, q_buf, kv_own, kv_far, k_0, k_1, k_2, k_3, v_0, v_1, v_2, v_3, send, row,
+    m_buf, acc_buf, bias_own, bias_near, bias_far, turning,
+    weight_sem, local_sem, out_sem, send_sem, recv_sem,
 ):
     sp = lax.axis_index("sp")
     tp = lax.axis_index("tp")
@@ -60,6 +60,58 @@
     own_blocks[0].start()
     own_blocks[1].start()
     own_tokens.start()
+    pl.semaphore_wait(barrier, len(peers))
+
+    copies = []
+
+    def remote(src, dst, peer):
+        at = len(copies)
+        copy = pltpu.make_async_remote_copy(
+            src_ref=src, dst_ref=dst, send_sem=send_sem.at[at], recv_sem=recv_sem.at[at],
+            device_id=peer, device_id_type=MESH,
+        )
+        copy.start()
+        copies.append(copy)
+        return copy
+
+    halves = (pl.ds(0, half), pl.ds(half, half))
+
+    class Spread:
+        def __init__(self, buf, source):
+            self.buf = buf
+            self.near = [
+                remote(source, buf.at[1, :, lane], x_up),
+                remote(source, buf.at[3, :, lane], x_down),
+                remote(source, buf.at[0, :, lane], sibling),
+            ]
+
+        def pass_near(self):
+            buf = self.buf
+            self.far = []
+            for part, back, peer in ((0, 1, x_up), (1, 3, x_down)):
+                self.near[part].wait_recv()
+                piece = halves[part]
+                self.far.append(remote(buf.at[back, piece, lane], buf.at[2, piece, lane], peer))
+            self.near_sibling = {
+                back: remote(buf.at[back, :, lane], buf.at[back, :, lane], sibling) for back in (1, 3)
+            }
+
+        def pass_far(self):
+            buf = self.buf
+            self.far_sibling = []
+            for part in range(2):
+                self.far[part].wait_recv()
+                piece = halves[part]
+                self.far_sibling.append(remote(buf.at[2, piece, lane], buf.at[2, piece, lane], sibling))
+
+    y_near = {0: [remote(cache_keys, held[1][0], y_up), remote(cache_keys, held[3][0], y_down)]}
+    own_spread = Spread(tok, tokens)
+    y_near[1] = [remote(cache_values, held[1][1], y_up), remote(cache_values, held[3][1], y_down)]
+    near_tokens = [
+        remote(tokens.at[halves[1], :], tok_near.at[0, halves[0], lane], after),
+        remote(tokens.at[halves[0], :], tok_near.at[0, halves[1], lane], before),
+    ]
+
     depth = 2 * width
     weight_copies = {}
     for back in (0, 1, 3, 2):
@@ -71,30 +123,10 @@
             copy.start()
             weight_copies[back, j] = copy
 
-    pl.semaphore_wait(barrier, len(peers))
-
-    copies = []
-
-    def remote(src, dst, peer):
-        at = len(copies)
-        copy = pltpu.make_async_remote_copy(
-            src_ref=src, dst_ref=dst, send_sem=send_sem.at[at], recv_sem=recv_sem.at[at],
-            device_id=peer, device_id_type=MESH,
-        )
-        copy.start()
-        copies.append(copy)
-        return copy
-
-    y_near = {0: [remote(cache_keys, held[1][0], y_up), remote(cache_keys, held[3][0], y_down)]}
-    x_from_down = remote(tokens, tok.at[1, :, lane], x_up)
-    x_from_up = remote(tokens, tok.at[3, :, lane], x_down)
-    from_sibling = remote(tokens, tok.at[0, :, lane], sibling)
-    y_near[1] = [remote(cache_values, held[1][1], y_up), remote(cache_values, held[3][1], y_down)]
-
     def wanted(holder, owner):
         local, found = jnp.int32(0), jnp.int32(0)
         for k in range(8):
-            block = window_map[owner, k]
+            block = window_map[k, owner]
             hit = jnp.where(block // 4 == holder, 1, 0)
             local = local + hit * (block % 4)
             found = found + hit
@@ -131,26 +163,29 @@
             remote(held[3][kv].at[high], held[2][kv].at[high], y_down),
         ]
 
-    def project(back, start):
-        for j in range(3):
-            weight_copies[back, j].wait()
-
-        @pl.loop(0, 3)
+    def project(buf, back, first, start):
+        @pl.loop(first, 3)
         def _(j):
-            columns = pl.ds(pl.multiple_of(j * width, HD), width)
-            product = jnp.dot(tok[back], weights[back, :, columns], preferred_element_type=f32)
+            source = pl.ds(pl.multiple_of(j * width, HD), width)
+            columns = pl.ds(pl.multiple_of((j - first) * width, HD), width)
+            product = jnp.dot(buf[back], weights[back, :, source], preferred_element_type=f32)
             if start:
                 total[:, columns] = product
             else:
                 total[:, columns] += product
 
+    def project_own(back, start=False):
+        for j in range(3):
+            weight_copies[back, j].wait()
+        project(tok, back, 0, start)
+
     for kv in range(2):
         own_blocks[kv].wait()
         z_send(kv, 0, 1)
 
     own_tokens.wait()
-    from_sibling.wait_recv()
-    project(0, True)
+    own_spread.near[2].wait_recv()
+    project_own(0, True)
 
     def radius_of(first, count):
         at = lax.broadcasted_iota(jnp.int32, (count, 1), 0) + first
@@ -169,32 +204,25 @@
 
     for part in range(2):
         first = part * half
-        bias_own[pl.ds(first, half), :] = bias_of(first, half, 0, rows, None)
-        left = rows - first
-        bias_halo[part, :, pl.ds(0, left)] = bias_of(first, half, first - rows, left, sp > 0)
-        bias_halo[part, :, pl.ds(left, half + first)] = bias_of(first, half, rows, half + first, sp < 15)
-
+        bias_own[halves[part], :] = bias_of(first, half, 0, rows, None)
+        bias_near[halves[part], halves[0]] = bias_of(first, half, -half, half, sp > 0)
+        bias_near[halves[part], halves[1]] = bias_of(first, half, rows, half, sp < 15)
+    bias_far[0] = bias_of(0, half, -rows, half, sp > 0)
+    bias_far[1] = bias_of(half, half, rows + half, half, sp < 15)
+
+    own_spread.pass_near()
     y_pass(0)
     z_send(0, 1, 2)
 
-    x_from_down.wait_recv()
-    x_far = [remote(tok.at[1, pl.ds(0, half), lane], tok.at[2, pl.ds(0, half), lane], x_up)]
-    x_from_up.wait_recv()
-    x_far.append(remote(tok.at[3, pl.ds(half, half), lane], tok.at[2, pl.ds(half, half), lane], x_down))
-    sibling_down = remote(tok.at[1, :, lane], tok.at[1, :, lane], sibling)
-    sibling_up = remote(tok.at[3, :, lane], tok.at[3, :, lane], sibling)
-    sibling_down.wait_recv()
-    project(1, False)
-    sibling_up.wait_recv()
-    project(3, False)
-    sibling_far = []
-    for part in range(2):
-        piece = pl.ds(part * half, half)
-        x_far[part].wait_recv()
-        sibling_far.append(remote(tok.at[2, piece, lane], tok.at[2, piece, lane], sibling))
-    for copy in sibling_far:
-        copy.wait_recv()
-    project(2, False)
+    for back in (1, 3):
+        own_spread.near_sibling[back].wait_recv()
+        project_own(back)
+    own_spread.pass_far()
+    y_pass(1)
+    z_send(1, 1, 2)
+    for copy in own_spread.far_sibling:
+        copy.wait_recv()
+    project_own(2)
 
     for h in range(heads):
         for j in range(3):
@@ -204,9 +232,7 @@
             else:
                 kv_own[j - 1, h] = part
 
-    y_pass(1)
-    z_send(1, 1, 2)
-    halo_copies = {}
+    far_copies = {}
     turns = []
 
     def describe(src, dst, send_at, recv_at, peer):
@@ -215,30 +241,35 @@
             device_id=peer, device_id_type=MESH,
         )
 
+    sides = ((0, after, 3, z_up, y_up), (1, before, 0, z_down, y_down))
     for h in range(heads):
-        halo_copies[h] = []
-        for side, peer in ((0, after), (1, before)):
-            halo_copies[h].append(remote(kv_own.at[0, h], halo.at[side, 0, h], peer))
-        turn_at = N_COPIES - 1 - h
-        for side, peer, last, z_next, y_next in ((0, after, 3, z_up, y_up), (1, before, 0, z_down, y_down)):
-            at = len(copies)
-            source, place = kv_own.at[1, h], halo.at[side, 1, h]
-            straight = describe(source, place, at, at, peer)
-            turn = describe(source, turning.at[h], at, turn_at, z_next)
-            onward = describe(turning.at[h], place, turn_at, at, y_next)
-            copies.append(straight)
-            halo_copies[h].append(straight)
-            turns.append((last, turn, onward))
-
-            @pl.when(y != last)
-            def _():
-                straight.start()
-
-            @pl.when(y == last)
-            def _():
-                turn.start()
-
-    def turn_values():
+        far_copies[h] = []
+        for kv in range(2):
+            turned = kv == 1 or h < 2
+            if turned:
+                slot = len(turns) // 2
+            for side, peer, last, z_next, y_next in sides:
+                source, place = kv_own.at[kv, h, halves[side]], kv_far.at[side, kv, h]
+                if not turned:
+                    far_copies[h].append(remote(source, place, peer))
+                    continue
+                at, turn_at = len(copies), N_COPIES - 1 - slot
+                straight = describe(source, place, at, at, peer)
+                turn = describe(source, turning.at[slot], at, turn_at, z_next)
+                onward = describe(turning.at[slot], place, turn_at, at, y_next)
+                copies.append(straight)
+                far_copies[h].append(straight)
+                turns.append((last, turn, onward))
+
+                @pl.when(y != last)
+                def _():
+                    straight.start()
+
+                @pl.when(y == last)
+                def _():
+                    turn.start()
+
+    def pass_turned():
         for last, turn, onward in turns:
 
             @pl.when(y == last)
@@ -294,40 +325,65 @@
             )
             attend(h, everything, scores, values, count)
 
+    def rows_of(part, bias, first=False):
+        for h in range(heads):
+            scores = lax.dot_general(q_buf[h], part(0, h), contract, preferred_element_type=f32)
+            attend(h, pl.ds(0, rows), scores + bias[...], part(1, h), 4, first)
+
+    rows_of(lambda kv, h: kv_own[kv, h], bias_own, first=True)
+
+    for copy in near_tokens:
+        copy.wait_recv()
+    near_spread = Spread(tok_near, tok_near.at[0, :, lane])
+    for copy in z_copies[0, 0] + z_copies[1, 0]:
+        copy.wait_recv()
+    slots(((0, 0), (0, 1), (0, 2), (1, 0), (2, 0), (3, 0)))
+    near_spread.near[2].wait_recv()
+    project(tok_near, 0, 1, True)
+
+    for copy in y_far[0]:
+        copy.wait_recv()
+    z_send(0, 3, 1)
+    for copy in y_far[1]:
+        copy.wait_recv()
+    z_send(1, 3, 1)
+
+    near_spread.pass_near()
+    for back in (1, 3):
+        near_spread.near_sibling[back].wait_recv()
+        project(tok_near, back, 1, False)
+    pass_turned()
+    near_spread.pass_far()
+    for copy in z_copies[0, 1] + z_copies[1, 1]:
+        copy.wait_recv()
+    slots(((1, 1), (1, 2), (2, 1), (2, 2), (3, 1), (3, 2)))
+    for copy in near_spread.far_sibling:
+        copy.wait_recv()
+    project(tok_near, 2, 1, False)
+    tok[0] = total[:, : 2 * width].astype(bf16)
+    rows_of(lambda kv, h: tok[0, :, pl.ds(kv * width + h * HD, HD)], bias_near)
+
     for h in range(heads):
-        scores = lax.dot_general(q_buf[h], kv_own[0, h], contract, preferred_element_type=f32)
-        attend(h, pl.ds(0, rows), scores + bias_own[...], kv_own[1, h], 4, first=True)
-
-    for copy in y_far[0]:
-        copy.wait_recv()
-    z_send(0, 3, 1)
-    for copy in z_copies[0, 0] + z_copies[1, 0]:
-        copy.wait_recv()
-    slots(((0, 0), (0, 1), (0, 2), (1, 0), (2, 0), (3, 0)))
-    for copy in y_far[1]:
-        copy.wait_recv()
-    z_send(1, 3, 1)
-    for copy in z_copies[0, 1] + z_copies[1, 1]:
-        copy.wait_recv()
-    slots(((1, 1), (1, 2), (2, 1), (2, 2), (3, 1), (3, 2)))
-    turn_values()
+        for copy in far_copies[h]:
+            copy.wait_recv()
+        for side in range(2):
+            at = halves[side]
+            scores = lax.dot_general(q_buf[h, at], kv_far[side, 0, h], contract, preferred_element_type=f32)
+            attend(h, at, scores + bias_far[side], kv_far[side, 1, h], 2)
+
     for copy in z_copies[0, 3] + z_copies[1, 3]:
         copy.wait_recv()
     slots(((0, 3), (1, 3), (2, 3), (3, 3)))
 
+    out_copies = []
     for h in range(heads):
-        for copy in halo_copies[h]:
-            copy.wait_recv()
-        for part in range(2):
-            at = pl.ds(part * half, half)
-            left = pl.ds(part * half, rows - part * half)
-            right = pl.ds(0, half + part * half)
-            keys = jnp.concatenate([halo[0, 0, h, left], halo[1, 0, h, right]], axis=0)
-            values = jnp.concatenate([halo[0, 1, h, left], halo[1, 1, h, right]], axis=0)
-            scores = lax.dot_general(q_buf[h, at], keys, contract, preferred_element_type=f32)
-            attend(h, at, scores + bias_halo[part], values, 6)
         sums = acc_buf[h]
-        out[:, pl.ds(h * HD, HD)] = (sums[:, :HD] / sums[:, HD:]).astype(out.dtype)
+        lanes = pl.ds(h * HD, HD)
+        q_buf[h] = (sums[:, :HD] / sums[:, HD:]).astype(out.dtype)
+        out_copies.append(pltpu.make_async_copy(q_buf.at[h], out.at[:, lanes], out_sem.at[h]))
+        out_copies[h].start()
+    for copy in out_copies:
+        copy.wait()
 
     for copy in copies:
         copy.wait_send()
@@ -347,14 +403,15 @@
         kernel,
         out_shape=jax.ShapeDtypeStruct((rows, width), bf16),
         in_specs=[pl.BlockSpec(memory_space=pl.ANY)] * 6 + [pl.BlockSpec(memory_space=pltpu.SMEM)] * 2,
-        out_specs=pl.BlockSpec(memory_space=pltpu.VMEM),
+        out_specs=pl.BlockSpec(memory_space=pl.ANY),
         scratch_shapes=[
+            pltpu.VMEM((4, rows, 2 * width), bf16),
             pltpu.VMEM((4, rows, 2 * width), bf16),
             pltpu.VMEM((4, 2 * width, 3 * width), bf16),
             pltpu.VMEM((rows, 3 * width), f32),
             pltpu.VMEM((heads, rows, HD), bf16),
             pltpu.VMEM((2, heads, rows, HD), bf16),
-            pltpu.VMEM((2, 2, heads, rows, HD), bf16),
+            pltpu.VMEM((2, 2, heads, rows // 2, HD), bf16),
             pltpu.VMEM((4,) + block, bf16),
             pltpu.VMEM((4,) + block, bf16),
             pltpu.VMEM((4,) + block, bf16),
@@ -368,17 +425,19 @@
             pltpu.VMEM((heads, rows, HD), f32),
             pltpu.VMEM((heads, rows, 2 * HD), f32),
             pltpu.VMEM((rows, rows), f32),
-            pltpu.VMEM((2, rows // 2, 3 * rows // 2), f32),
-            pltpu.VMEM((heads, rows, HD), bf16),
+            pltpu.VMEM((rows, rows), f32),
+            pltpu.VMEM((2, rows // 2, rows // 2), f32),
+            pltpu.VMEM((7, rows // 2, HD), bf16),
             pltpu.SemaphoreType.DMA((4, 3)),
             pltpu.SemaphoreType.DMA((3,)),
+            pltpu.SemaphoreType.DMA((heads,)),
             pltpu.SemaphoreType.DMA((N_COPIES,)),
             pltpu.SemaphoreType.DMA((N_COPIES,)),
         ],
         compiler_params=pltpu.CompilerParams(
-            collective_id=0, has_side_effects=True, vmem_limit_bytes=62 * 1024 * 1024
+            collective_id=0, has_side_effects=True, vmem_limit_bytes=63 * 1024 * 1024
         ),
-    )(tokens, w_query, w_key, w_value, cache_keys, cache_values, tile_level, window_map)
+    )(tokens, w_query, w_key, w_value, cache_keys, cache_values, tile_level, window_map.T)
 
 
 def solution(mesh):

time: 97.9 us -> 87.4 us (0.89)
  Pallas kernels: 93.5 us -> 83.7 us
  local copies, waits for them, and re-layouts: 3.33 us -> 1.98 us
    pallas_call x1, Pallas kernels: 93.5 us -> 83.7 us  [body(): pl.pallas_call(kernel, out_shape=jax.ShapeDtypeStruct((rows, width), bf16...]
    unnamed x2 -> x1, local copies, waits for them, and re-layouts: 3.33 us -> 1.98 us
where the time goes in v3:
time: 87.4 us; the launch traced here: 85.7 us
  Pallas kernels  83.7 us (96%)
  local copies, waits for them, and re-layouts  1.98 us (2%)
    pallas_call x1, Pallas kernels, body(): pl.pallas_call(kernel, out_shape=jax.ShapeDtypeStruct((rows, width), bf16...  83.7 us
    unnamed x1, local copies, waits for them, and re-layouts  1.98 us

profile of v3, /device:TPU:0, one launch (start us, length us, event | category | flops | bytes accessed | tf_op | source)
XLA Modules:
  0.0 85.7 jit_solution(7032277064498348591)
XLA Ops:
  0.0 83.7 %shard_map.82 = bf16[512,640]{1,0:T(8,128)(2,1)} custom-call(bf16[512,640]{1,0:T(8,128)(2,1)} %tokens.1, bf16[5120,640]{1,0:T(8,128)(2,1)} %w_query.1, bf16[5120,640]{1,0:T(8,128)(2,1)} %w_key.1, bf16[5120,640]{1,0:T(8,128)(2,1)} %w_value.1, bf16[4,128,640]{2,1,0:T(8,128)(2,1)} %cache_keys.1, bf16[4,128,640]{2,1,0:T(8,128)(2,1)} %cache_values.1, ...), custom_call_target="tpu_custom_call" | custom-call | tf_op jit(solution)/shard_map/pallas_call | solution.py:402
  83.7 2.0 %copy.10 = bf16[512,640]{1,0:T(8,128)(2,1)} copy(bf16[512,640]{1,0:T(8,128)(2,1)} %shard_map.82) | data formatting | bytes 1310720

commit v4 on v3

--- a/solution.py
+++ b/solution.py
@@ -15,7 +15,7 @@
 LOW = -1e30
 SCALE = math.log2(math.e) / math.sqrt(HD)
 COLUMN = (0, 1, 3, 2)
-N_COPIES = 96
+N_COPIES = 60
 
 
 def kernel(
@@ -106,11 +106,11 @@
 
     y_near = {0: [remote(cache_keys, held[1][0], y_up), remote(cache_keys, held[3][0], y_down)]}
     own_spread = Spread(tok, tokens)
-    y_near[1] = [remote(cache_values, held[1][1], y_up), remote(cache_values, held[3][1], y_down)]
     near_tokens = [
         remote(tokens.at[halves[1], :], tok_near.at[0, halves[0], lane], after),
         remote(tokens.at[halves[0], :], tok_near.at[0, halves[1], lane], before),
     ]
+    y_near[1] = [remote(cache_values, held[1][1], y_up), remote(cache_values, held[3][1], y_down)]
 
     depth = 2 * width
     weight_copies = {}
@@ -164,10 +164,10 @@
         ]
 
     def project(buf, back, first, start):
-        @pl.loop(first, 3)
-        def _(j):
-            source = pl.ds(pl.multiple_of(j * width, HD), width)
-            columns = pl.ds(pl.multiple_of((j - first) * width, HD), width)
+        wide = (3 - first) * width
+        for at in range(0, wide, 2 * HD):
+            columns = pl.ds(at, min(2 * HD, wide - at))
+            source = pl.ds(first * width + at, min(2 * HD, wide - at))
             product = jnp.dot(buf[back], weights[back, :, source], preferred_element_type=f32)
             if start:
                 total[:, columns] = product
@@ -218,8 +218,9 @@
         own_spread.near_sibling[back].wait_recv()
         project_own(back)
     own_spread.pass_far()
-    y_pass(1)
-    z_send(1, 1, 2)
+    for copy in near_tokens:
+        copy.wait_recv()
+    near_spread = Spread(tok_near, tok_near.at[0, :, lane])
     for copy in own_spread.far_sibling:
         copy.wait_recv()
     project_own(2)
@@ -232,7 +233,7 @@
             else:
                 kv_own[j - 1, h] = part
 
-    far_copies = {}
+    far_copies = []
     turns = []
 
     def describe(src, dst, send_at, recv_at, peer):
@@ -242,35 +243,37 @@
         )
 
     sides = ((0, after, 3, z_up, y_up), (1, before, 0, z_down, y_down))
-    for h in range(heads):
-        far_copies[h] = []
-        for kv in range(2):
-            turned = kv == 1 or h < 2
-            if turned:
-                slot = len(turns) // 2
-            for side, peer, last, z_next, y_next in sides:
-                source, place = kv_own.at[kv, h, halves[side]], kv_far.at[side, kv, h]
-                if not turned:
-                    far_copies[h].append(remote(source, place, peer))
-                    continue
-                at, turn_at = len(copies), N_COPIES - 1 - slot
-                straight = describe(source, place, at, at, peer)
-                turn = describe(source, turning.at[slot], at, turn_at, z_next)
-                onward = describe(turning.at[slot], place, turn_at, at, y_next)
-                copies.append(straight)
-                far_copies[h].append(straight)
-                turns.append((last, turn, onward))
-
-                @pl.when(y != last)
-                def _():
-                    straight.start()
-
-                @pl.when(y == last)
-                def _():
-                    turn.start()
+    turned = ((0, 0, 2), (1, 0, 2), (1, 2, 3))
+    for slot, (kv, first, count) in enumerate(turned):
+        some_heads = pl.ds(first, count)
+        for side, peer, last, z_next, y_next in sides:
+            source, place = kv_own.at[kv, some_heads, halves[side]], kv_far.at[side, kv, some_heads]
+            at, turn_at = len(copies), N_COPIES - 1 - slot
+            staged = turning.at[pl.ds((0, 2, 4)[slot], count)]
+            straight = describe(source, place, at, at, peer)
+            turn = describe(source, staged, at, turn_at, z_next)
+            onward = describe(staged, place, turn_at, at, y_next)
+            copies.append(straight)
+            far_copies.append(straight)
+            turns.append((last, straight, turn, onward))
+
+            @pl.when(y == last)
+            def _():
+                turn.start()
+
+    def send_straight():
+        for last, straight, _, _ in turns:
+
+            @pl.when(y != last)
+            def _():
+                straight.start()
+
+        for side, peer, _, _, _ in sides:
+            source, place = kv_own.at[0, pl.ds(2, 3), halves[side]], kv_far.at[side, 0, pl.ds(2, 3)]
+            far_copies.append(remote(source, place, peer))
 
     def pass_turned():
-        for last, turn, onward in turns:
+        for last, _, turn, onward in turns:
 
             @pl.when(y == last)
             def _():
@@ -278,22 +281,29 @@
                 onward.start()
 
     ones = jnp.ones((BLOCK, HD), bf16)
-
-    def attend(h, at, scores, values, count, first=False):
+    everything = pl.ds(0, rows)
+
+    def weigh(h, at, scores, count, first=False):
         pieces = [scores[:, i * BLOCK : (i + 1) * BLOCK] for i in range(count)]
         top = functools.reduce(jnp.maximum, pieces)
         top = jnp.broadcast_to(jnp.max(top, axis=1, keepdims=True), pieces[0].shape)
+        keep = None
         if not first:
             old = m_buf[h, at]
             top = jnp.maximum(top, old)
             keep = jnp.exp2((old - top) * SCALE)
+        m_buf[h, at] = top
         scaled = top * SCALE
-        weight = jnp.concatenate(
-            [jnp.exp2(piece * SCALE - scaled).astype(bf16) for piece in pieces], axis=1
-        )
-        values = jnp.concatenate([values, jnp.concatenate([ones] * count, axis=0)], axis=1)
-        mixed = jnp.dot(weight, values, preferred_element_type=f32)
-        m_buf[h, at] = top
+        return [jnp.exp2(piece * SCALE - scaled) for piece in pieces], keep
+
+    def mix(pieces, values):
+        weight = jnp.concatenate([piece.astype(bf16) for piece in pieces], axis=1)
+        values = jnp.concatenate([values, jnp.concatenate([ones] * len(pieces), axis=0)], axis=1)
+        return jnp.dot(weight, values, preferred_element_type=f32)
+
+    def attend(h, at, scores, values, count, first=False):
+        pieces, keep = weigh(h, at, scores, count, first)
+        mixed = mix(pieces, values)
         for side in range(2):
             lanes = pl.ds(side * HD, HD)
             part = mixed[:, side * HD : (side + 1) * HD]
@@ -301,9 +311,7 @@
 
     contract = (((1,), (1,)), ((), ()))
 
-    def slots(places):
-        everything = pl.ds(0, rows)
-        count = len(places)
+    def slot_scores(places):
         first_lane = lax.broadcasted_iota(jnp.int32, (BLOCK, HD), 1) == 0
         bias = []
         for back, position in places:
@@ -314,70 +322,82 @@
         bias = jnp.concatenate(bias, axis=0)
         pointer = jnp.where(lax.broadcasted_iota(jnp.int32, (rows, HD), 1) == 0, 1.0, 0.0).astype(bf16)
         for h in range(heads):
-            lanes = pl.ds(h * HD, HD)
-            keys = jnp.concatenate([row[0, b, p, :, lanes] for b, p in places], axis=0)
-            values = jnp.concatenate([row[1, b, p, :, lanes] for b, p in places], axis=0)
-            scores = lax.dot_general(
+            keys = slot_rows(0, h, places)
+            yield h, lax.dot_general(
                 jnp.concatenate([q_buf[h], pointer], axis=1),
                 jnp.concatenate([keys, bias], axis=1),
                 contract,
                 preferred_element_type=f32,
             )
-            attend(h, everything, scores, values, count)
+
+    def slot_rows(kv, h, places):
+        return jnp.concatenate([row[kv, b, p, :, pl.ds(h * HD, HD)] for b, p in places], axis=0)
+
+    def slots(places):
+        for h, scores in slot_scores(places):
+            attend(h, everything, scores, slot_rows(1, h, places), len(places))
 
     def rows_of(part, bias, first=False):
         for h in range(heads):
             scores = lax.dot_general(q_buf[h], part(0, h), contract, preferred_element_type=f32)
             attend(h, pl.ds(0, rows), scores + bias[...], part(1, h), 4, first)
 
-    rows_of(lambda kv, h: kv_own[kv, h], bias_own, first=True)
-
-    for copy in near_tokens:
-        copy.wait_recv()
-    near_spread = Spread(tok_near, tok_near.at[0, :, lane])
-    for copy in z_copies[0, 0] + z_copies[1, 0]:
-        copy.wait_recv()
-    slots(((0, 0), (0, 1), (0, 2), (1, 0), (2, 0), (3, 0)))
     near_spread.near[2].wait_recv()
     project(tok_near, 0, 1, True)
-
-    for copy in y_far[0]:
-        copy.wait_recv()
-    z_send(0, 3, 1)
-    for copy in y_far[1]:
-        copy.wait_recv()
-    z_send(1, 3, 1)
+    rows_of(lambda kv, h: kv_own[kv, h], bias_own, first=True)
+    for copy in z_copies[0, 0] + z_copies[1, 0]:
+        copy.wait_recv()
+    y_pass(1)
+    z_send(1, 1, 2)
+    send_straight()
+    slots(((0, 0), (0, 1), (0, 2), (1, 0), (2, 0), (3, 0)))
 
     near_spread.pass_near()
     for back in (1, 3):
         near_spread.near_sibling[back].wait_recv()
         project(tok_near, back, 1, False)
+    for copy in y_far[0]:
+        copy.wait_recv()
+    z_send(0, 3, 1)
     pass_turned()
     near_spread.pass_far()
-    for copy in z_copies[0, 1] + z_copies[1, 1]:
-        copy.wait_recv()
-    slots(((1, 1), (1, 2), (2, 1), (2, 2), (3, 1), (3, 2)))
+    for copy in y_far[1]:
+        copy.wait_recv()
+    z_send(1, 3, 1)
     for copy in near_spread.far_sibling:
         copy.wait_recv()
     project(tok_near, 2, 1, False)
     tok[0] = total[:, : 2 * width].astype(bf16)
     rows_of(lambda kv, h: tok[0, :, pl.ds(kv * width + h * HD, HD)], bias_near)
-
+    for copy in z_copies[0, 1] + z_copies[1, 1]:
+        copy.wait_recv()
+    slots(((1, 1), (1, 2), (2, 1), (2, 2), (3, 1), (3, 2), (0, 3)))
+
+    for copy in far_copies:
+        copy.wait_recv()
     for h in range(heads):
-        for copy in far_copies[h]:
-            copy.wait_recv()
         for side in range(2):
             at = halves[side]
             scores = lax.dot_general(q_buf[h, at], kv_far[side, 0, h], contract, preferred_element_type=f32)
             attend(h, at, scores + bias_far[side], kv_far[side, 1, h], 2)
 
-    for copy in z_copies[0, 3] + z_copies[1, 3]:
-        copy.wait_recv()
-    slots(((0, 3), (1, 3), (2, 3), (3, 3)))
-
+    last_places = ((1, 3), (2, 3), (3, 3))
+    span = len(last_places) * BLOCK
+    for copy in z_copies[0, 3]:
+        copy.wait_recv()
+    for h, scores in slot_scores(last_places):
+        pieces, keep = weigh(h, everything, scores, len(last_places))
+        for i, piece in enumerate(pieces):
+            total[:, pl.ds(h * span + i * BLOCK, BLOCK)] = piece
+        for side in range(2):
+            lanes = pl.ds(side * HD, HD)
+            acc_buf[h, :, lanes] = acc_buf[h, :, lanes] * keep
+    for copy in z_copies[1, 3]:
+        copy.wait_recv()
     out_copies = []
     for h in range(heads):
-        sums = acc_buf[h]
+        pieces = [total[:, pl.ds(h * span + i * BLOCK, BLOCK)] for i in range(len(last_places))]
+        sums = acc_buf[h] + mix(pieces, slot_rows(1, h, last_places))
         lanes = pl.ds(h * HD, HD)
         q_buf[h] = (sums[:, :HD] / sums[:, HD:]).astype(out.dtype)
         out_copies.append(pltpu.make_async_copy(q_buf.at[h], out.at[:, lanes], out_sem.at[h]))
@@ -385,9 +405,10 @@
     for copy in out_copies:
         copy.wait()
 
+    assert len(copies) <= N_COPIES - 3
     for copy in copies:
         copy.wait_send()
-    for last, _, onward in turns:
+    for last, _, _, onward in turns:
 
         @pl.when(y == last)
         def _():

time: 87.4 us -> 84.9 us (0.971)
  Pallas kernels: 83.7 us -> 81.8 us
    pallas_call x1, Pallas kernels: 83.7 us -> 81.8 us  [body(): pl.pallas_call(kernel, out_shape=jax.ShapeDtypeStruct((rows, width), bf16...]
where the time goes in v4:
time: 84.9 us; the launch traced here: 83.8 us
  Pallas kernels  81.8 us (96%)
  local copies, waits for them, and re-layouts  1.98 us (2%)
    pallas_call x1, Pallas kernels, body(): pl.pallas_call(kernel, out_shape=jax.ShapeDtypeStruct((rows, width), bf16...  81.8 us
    unnamed x1, local copies, waits for them, and re-layouts  1.98 us

profile of v4, /device:TPU:0, one launch (start us, length us, event | category | flops | bytes accessed | tf_op | source)
XLA Modules:
  0.0 83.8 jit_solution(3835574676008272170)
XLA Ops:
  0.0 81.8 %shard_map.82 = bf16[512,640]{1,0:T(8,128)(2,1)} custom-call(bf16[512,640]{1,0:T(8,128)(2,1)} %tokens.1, bf16[5120,640]{1,0:T(8,128)(2,1)} %w_query.1, bf16[5120,640]{1,0:T(8,128)(2,1)} %w_key.1, bf16[5120,640]{1,0:T(8,128)(2,1)} %w_value.1, bf16[4,128,640]{2,1,0:T(8,128)(2,1)} %cache_keys.1, bf16[4,128,640]{2,1,0:T(8,128)(2,1)} %cache_values.1, ...), custom_call_target="tpu_custom_call" | custom-call | tf_op jit(solution)/shard_map/pallas_call | solution.py:423
  81.8 2.0 %copy.10 = bf16[512,640]{1,0:T(8,128)(2,1)} copy(bf16[512,640]{1,0:T(8,128)(2,1)} %shard_map.82) | data formatting | bytes 1310720

commit v5 on v4

--- a/solution.py
+++ b/solution.py
@@ -45,11 +45,18 @@
     after = ((sp + 1) % 16, tp)
     before = ((sp + 15) % 16, tp)
     held = ((k_0, v_0), (k_1, v_1), (k_2, v_2), (k_3, v_3))
-    peers = (sibling, x_up, x_down, y_up, y_down, z_up, z_down, z_far, after, before)
+    peers = (sibling, x_up, x_down, y_up, y_down, z_up, z_down, z_far)
+    has_after, has_before = sp < 15, sp > 0
+    far_after, far_before = has_after & (y == 3), has_before & (y == 0)
 
     barrier = pltpu.get_barrier_semaphore()
     for peer in peers:
         pl.semaphore_signal(barrier, inc=1, device_id=peer, device_id_type=MESH)
+    for far, peer in ((far_after, after), (far_before, before)):
+
+        @pl.when(far)
+        def _():
+            pl.semaphore_signal(barrier, inc=1, device_id=peer, device_id_type=MESH)
 
     lane = pl.ds(pl.multiple_of(core * width, HD), width)
     own_tokens = pltpu.make_async_copy(tokens, tok.at[0, :, lane], local_sem.at[0])
@@ -60,19 +67,41 @@
     own_blocks[0].start()
     own_blocks[1].start()
     own_tokens.start()
-    pl.semaphore_wait(barrier, len(peers))
+    pl.semaphore_wait(barrier, len(peers) + far_after.astype(jnp.int32) + far_before.astype(jnp.int32))
 
     copies = []
+
+    def describe(src, dst, send_at, recv_at, peer):
+        return pltpu.make_async_remote_copy(
+            src_ref=src, dst_ref=dst, send_sem=send_sem.at[send_at], recv_sem=recv_sem.at[recv_at],
+            device_id=peer, device_id_type=MESH,
+        )
 
     def remote(src, dst, peer):
         at = len(copies)
-        copy = pltpu.make_async_remote_copy(
-            src_ref=src, dst_ref=dst, send_sem=send_sem.at[at], recv_sem=recv_sem.at[at],
-            device_id=peer, device_id_type=MESH,
-        )
+        copy = describe(src, dst, at, at, peer)
         copy.start()
-        copies.append(copy)
+        copies.append((None, copy))
         return copy
+
+    sent = (has_after, has_before)
+    received = (has_before, has_after)
+
+    def prepare(src, dst, side):
+        at = len(copies)
+        copy = describe(src, dst, at, at, (after, before)[side])
+        copies.append((sent[side], copy))
+        return copy
+
+    def start_where(condition, copy):
+        @pl.when(condition)
+        def _():
+            copy.start()
+
+    def wait_for_side(side, copy):
+        @pl.when(received[side])
+        def _():
+            copy.wait_recv()
 
     halves = (pl.ds(0, half), pl.ds(half, half))
 
@@ -107,9 +136,10 @@
     y_near = {0: [remote(cache_keys, held[1][0], y_up), remote(cache_keys, held[3][0], y_down)]}
     own_spread = Spread(tok, tokens)
     near_tokens = [
-        remote(tokens.at[halves[1], :], tok_near.at[0, halves[0], lane], after),
-        remote(tokens.at[halves[0], :], tok_near.at[0, halves[1], lane], before),
+        prepare(tokens.at[halves[1 - side], :], tok_near.at[0, halves[side], lane], side) for side in range(2)
     ]
+    for side in range(2):
+        start_where(sent[side], near_tokens[side])
     y_near[1] = [remote(cache_values, held[1][1], y_up), remote(cache_values, held[3][1], y_down)]
 
     depth = 2 * width
@@ -179,6 +209,13 @@
             weight_copies[back, j].wait()
         project(tok, back, 0, start)
 
+    for side in range(2):
+
+        @pl.when(jnp.logical_not(received[side]))
+        def _():
+            tok_near[0, halves[side], lane] = jnp.zeros((half, width), bf16)
+            kv_far[side] = jnp.zeros_like(kv_far[side])
+
     for kv in range(2):
         own_blocks[kv].wait()
         z_send(kv, 0, 1)
@@ -218,8 +255,8 @@
         own_spread.near_sibling[back].wait_recv()
         project_own(back)
     own_spread.pass_far()
-    for copy in near_tokens:
-        copy.wait_recv()
+    for side in range(2):
+        wait_for_side(side, near_tokens[side])
     near_spread = Spread(tok_near, tok_near.at[0, :, lane])
     for copy in own_spread.far_sibling:
         copy.wait_recv()
@@ -235,47 +272,34 @@
 
     far_copies = []
     turns = []
-
-    def describe(src, dst, send_at, recv_at, peer):
-        return pltpu.make_async_remote_copy(
-            src_ref=src, dst_ref=dst, send_sem=send_sem.at[send_at], recv_sem=recv_sem.at[recv_at],
-            device_id=peer, device_id_type=MESH,
-        )
-
-    sides = ((0, after, 3, z_up, y_up), (1, before, 0, z_down, y_down))
+    last_ones = ((y == 3, z_up, y_up, z > 0), (y == 0, z_down, y_down, z < 3))
     turned = ((0, 0, 2), (1, 0, 2), (1, 2, 3))
     for slot, (kv, first, count) in enumerate(turned):
         some_heads = pl.ds(first, count)
-        for side, peer, last, z_next, y_next in sides:
+        for side in range(2):
+            last, z_next, y_next, comes = last_ones[side]
             source, place = kv_own.at[kv, some_heads, halves[side]], kv_far.at[side, kv, some_heads]
             at, turn_at = len(copies), N_COPIES - 1 - slot
             staged = turning.at[pl.ds((0, 2, 4)[slot], count)]
-            straight = describe(source, place, at, at, peer)
+            straight = prepare(source, place, side)
+            far_copies.append((side, straight))
             turn = describe(source, staged, at, turn_at, z_next)
             onward = describe(staged, place, turn_at, at, y_next)
-            copies.append(straight)
-            far_copies.append(straight)
-            turns.append((last, straight, turn, onward))
-
-            @pl.when(y == last)
-            def _():
-                turn.start()
+            turns.append((sent[side] & jnp.logical_not(last), straight, last & comes, turn, onward))
+            start_where(sent[side] & last, turn)
 
     def send_straight():
-        for last, straight, _, _ in turns:
-
-            @pl.when(y != last)
-            def _():
-                straight.start()
-
-        for side, peer, _, _, _ in sides:
-            source, place = kv_own.at[0, pl.ds(2, 3), halves[side]], kv_far.at[side, 0, pl.ds(2, 3)]
-            far_copies.append(remote(source, place, peer))
+        for here, straight, _, _, _ in turns:
+            start_where(here, straight)
+        for side in range(2):
+            copy = prepare(kv_own.at[0, pl.ds(2, 3), halves[side]], kv_far.at[side, 0, pl.ds(2, 3)], side)
+            far_copies.append((side, copy))
+            start_where(sent[side], copy)
 
     def pass_turned():
-        for last, _, turn, onward in turns:
-
-            @pl.when(y == last)
+        for _, _, here, turn, onward in turns:
+
+            @pl.when(here)
             def _():
                 turn.wait_recv()
                 onward.start()
@@ -373,8 +397,8 @@
         copy.wait_recv()
     slots(((1, 1), (1, 2), (2, 1), (2, 2), (3, 1), (3, 2), (0, 3)))
 
-    for copy in far_copies:
-        copy.wait_recv()
+    for side, copy in far_copies:
+        wait_for_side(side, copy)
     for h in range(heads):
         for side in range(2):
             at = halves[side]
@@ -406,11 +430,18 @@
         copy.wait()
 
     assert len(copies) <= N_COPIES - 3
-    for copy in copies:
-        copy.wait_send()
-    for last, _, _, onward in turns:
-
-        @pl.when(y == last)
+    for condition, copy in copies:
+        if condition is None:
+            copy.wait_send()
+        else:
+
+            @pl.when(condition)
+            def _():
+                copy.wait_send()
+
+    for _, _, here, _, onward in turns:
+
+        @pl.when(here)
         def _():
             onward.wait_send()
 

time: 84.9 us -> 82.3 us (0.969); the launches traced: 83.8 us -> 82.1 us
  Pallas kernels: 81.8 us -> 80.1 us
    pallas_call x1, Pallas kernels: 81.8 us -> 80.1 us  [body(): pl.pallas_call(kernel, out_shape=jax.ShapeDtypeStruct((rows, width), bf16...]
where the time goes in v5:
time: 82.3 us; the launch traced here: 82.1 us
  Pallas kernels  80.1 us (97%)
  local copies, waits for them, and re-layouts  1.98 us (2%)
    pallas_call x1, Pallas kernels, body(): pl.pallas_call(kernel, out_shape=jax.ShapeDtypeStruct((rows, width), bf16...  80.1 us
    unnamed x1, local copies, waits for them, and re-layouts  1.98 us

profile of v5, /device:TPU:0, one launch (start us, length us, event | category | flops | bytes accessed | tf_op | source)
XLA Modules:
  0.0 82.1 jit_solution(10767005138041682441)
XLA Ops:
  0.0 80.1 %shard_map.82 = bf16[512,640]{1,0:T(8,128)(2,1)} custom-call(bf16[512,640]{1,0:T(8,128)(2,1)} %tokens.1, bf16[5120,640]{1,0:T(8,128)(2,1)} %w_query.1, bf16[5120,640]{1,0:T(8,128)(2,1)} %w_key.1, bf16[5120,640]{1,0:T(8,128)(2,1)} %w_value.1, bf16[4,128,640]{2,1,0:T(8,128)(2,1)} %cache_keys.1, bf16[4,128,640]{2,1,0:T(8,128)(2,1)} %cache_values.1, ...), custom_call_target="tpu_custom_call" | custom-call | tf_op jit(solution)/shard_map/pallas_call | solution.py:454
  80.1 2.0 %copy.10 = bf16[512,640]{1,0:T(8,128)(2,1)} copy(bf16[512,640]{1,0:T(8,128)(2,1)} %shard_map.82) | data formatting | bytes 1310720

commit v6 on v5

--- a/solution.py
+++ b/solution.py
@@ -15,13 +15,13 @@
 LOW = -1e30
 SCALE = math.log2(math.e) / math.sqrt(HD)
 COLUMN = (0, 1, 3, 2)
-N_COPIES = 60
+N_COPIES = 66
 
 
 def kernel(
     tokens, w_query, w_key, w_value, cache_keys, cache_values, tile_level, window_map,
     out,
-    tok, tok_near, weights, total, q_buf, kv_own, kv_far, k_0, k_1, k_2, k_3, v_0, v_1, v_2, v_3, send, row,
+    tok, tok_near, weights, total, q_buf, kv_own, kv_far, k_0, k_1, k_2, k_3, k_1b, k_3b, v_0, v_1, v_2, v_3, send, row,
     m_buf, acc_buf, bias_own, bias_near, bias_far, turning,
     weight_sem, local_sem, out_sem, send_sem, recv_sem,
 ):
@@ -45,6 +45,8 @@
     after = ((sp + 1) % 16, tp)
     before = ((sp + 15) % 16, tp)
     held = ((k_0, v_0), (k_1, v_1), (k_2, v_2), (k_3, v_3))
+    cuts = (pl.ds(0, 3 * HD), pl.ds(3 * HD, width - 3 * HD))
+    cut_keys = {1: (k_1, k_1b), 3: (k_3, k_3b)}
     peers = (sibling, x_up, x_down, y_up, y_down, z_up, z_down, z_far)
     has_after, has_before = sp < 15, sp > 0
     far_after, far_before = has_after & (y == 3), has_before & (y == 0)
@@ -133,8 +135,13 @@
                 piece = halves[part]
                 self.far_sibling.append(remote(buf.at[2, piece, lane], buf.at[2, piece, lane], sibling))
 
-    y_near = {0: [remote(cache_keys, held[1][0], y_up), remote(cache_keys, held[3][0], y_down)]}
-    own_spread = Spread(tok, tokens)
+    y_near = {}
+    near_keys = []
+    for part in range(2):
+        source = cache_keys.at[:, :, cuts[part]]
+        near_keys.append([remote(source, cut_keys[1][part], y_up), remote(source, cut_keys[3][part], y_down)])
+        if part == 0:
+            own_spread = Spread(tok, tokens)
     near_tokens = [
         prepare(tokens.at[halves[1 - side], :], tok_near.at[0, halves[side], lane], side) for side in range(2)
     ]
@@ -184,6 +191,32 @@
 
     y_far = {}
 
+    def pass_keys(part):
+        cut = cuts[part]
+        for copy in near_keys[part]:
+            copy.wait_recv()
+        low, high = pl.ds(0, 2), pl.ds(2, 2)
+        y_far.setdefault(0, []).extend([
+            remote(cut_keys[1][part].at[low], held[2][0].at[low, :, cut], y_up),
+            remote(cut_keys[3][part].at[high], held[2][0].at[high, :, cut], y_down),
+        ])
+        for position in (1, 2):
+            column = COLUMN[position]
+            holder = z * 4 + (y + 4 - column) % 4
+            for step in range(4):
+                local, _ = wanted(holder, ((z + step) % 4) * 4 + y)
+                block = cut_keys[column][part][local]
+                if step == 0:
+                    row[0, 0, position, :, cut] = block
+                else:
+                    send[0, step - 1, position, :, cut] = block
+        slots = pl.ds(1, 2)
+        z_copies.setdefault((0, 1), []).extend([
+            remote(send.at[0, 1, slots, :, cut], row.at[0, 2, slots, :, cut], z_far),
+            remote(send.at[0, 0, slots, :, cut], row.at[0, 1, slots, :, cut], z_up),
+            remote(send.at[0, 2, slots, :, cut], row.at[0, 3, slots, :, cut], z_down),
+        ])
+
     def y_pass(kv):
         low, high = pl.ds(0, 2), pl.ds(2, 2)
         for copy in y_near[kv]:
@@ -247,9 +280,9 @@
     bias_far[0] = bias_of(0, half, -rows, half, sp > 0)
     bias_far[1] = bias_of(half, half, rows + half, half, sp < 15)
 
+    pass_keys(0)
     own_spread.pass_near()
-    y_pass(0)
-    z_send(0, 1, 2)
+    pass_keys(1)
 
     for back in (1, 3):
         own_spread.near_sibling[back].wait_recv()
@@ -273,14 +306,14 @@
     far_copies = []
     turns = []
     last_ones = ((y == 3, z_up, y_up, z > 0), (y == 0, z_down, y_down, z < 3))
-    turned = ((0, 0, 2), (1, 0, 2), (1, 2, 3))
+    turned = ((0, 0, 3), (1, 0, 2), (1, 2, 3))
     for slot, (kv, first, count) in enumerate(turned):
         some_heads = pl.ds(first, count)
         for side in range(2):
             last, z_next, y_next, comes = last_ones[side]
             source, place = kv_own.at[kv, some_heads, halves[side]], kv_far.at[side, kv, some_heads]
             at, turn_at = len(copies), N_COPIES - 1 - slot
-            staged = turning.at[pl.ds((0, 2, 4)[slot], count)]
+            staged = turning.at[pl.ds((0, 3, 5)[slot], count)]
             straight = prepare(source, place, side)
             far_copies.append((side, straight))
             turn = describe(source, staged, at, turn_at, z_next)
@@ -292,7 +325,7 @@
         for here, straight, _, _, _ in turns:
             start_where(here, straight)
         for side in range(2):
-            copy = prepare(kv_own.at[0, pl.ds(2, 3), halves[side]], kv_far.at[side, 0, pl.ds(2, 3)], side)
+            copy = prepare(kv_own.at[0, pl.ds(3, 2), halves[side]], kv_far.at[side, 0, pl.ds(3, 2)], side)
             far_copies.append((side, copy))
             start_where(sent[side], copy)
 
@@ -465,9 +498,11 @@
             pltpu.VMEM((2, heads, rows, HD), bf16),
             pltpu.VMEM((2, 2, heads, rows // 2, HD), bf16),
             pltpu.VMEM((4,) + block, bf16),
+            pltpu.VMEM((4, BLOCK, 3 * HD), bf16),
             pltpu.VMEM((4,) + block, bf16),
-            pltpu.VMEM((4,) + block, bf16),
-            pltpu.VMEM((4,) + block, bf16),
+            pltpu.VMEM((4, BLOCK, 3 * HD), bf16),
+            pltpu.VMEM((4, BLOCK, width - 3 * HD), bf16),
+            pltpu.VMEM((4, BLOCK, width - 3 * HD), bf16),
             pltpu.VMEM((4,) + block, bf16),
             pltpu.VMEM((4,) + block, bf16),
             pltpu.VMEM((4,) + block, bf16),
@@ -479,7 +514,7 @@
             pltpu.VMEM((rows, rows), f32),
             pltpu.VMEM((rows, rows), f32),
             pltpu.VMEM((2, rows // 2, rows // 2), f32),
-            pltpu.VMEM((7, rows // 2, HD), bf16),
+            pltpu.VMEM((8, rows // 2, HD), bf16),
             pltpu.SemaphoreType.DMA((4, 3)),
             pltpu.SemaphoreType.DMA((3,)),
             pltpu.SemaphoreType.DMA((heads,)),

time: 82.3 us -> 82.1 us (level)
  Pallas kernels: 80.1 us -> 79.2 us
    pallas_call x1, Pallas kernels: 80.1 us -> 79.2 us  [body(): pl.pallas_call(kernel, out_shape=jax.ShapeDtypeStruct((rows, width), bf16...]
where the time goes in v6:
time: 82.1 us; the launch traced here: 81.2 us
  Pallas kernels  79.2 us (96%)
  local copies, waits for them, and re-layouts  1.98 us (2%)
    pallas_call x1, Pallas kernels, body(): pl.pallas_call(kernel, out_shape=jax.ShapeDtypeStruct((rows, width), bf16...  79.2 us
    unnamed x1, local copies, waits for them, and re-layouts  1.98 us

profile of v6, /device:TPU:0, one launch (start us, length us, event | category | flops | bytes accessed | tf_op | source)
XLA Modules:
  0.0 81.2 jit_solution(6919805230027065100)
XLA Ops:
  0.0 79.2 %shard_map.82 = bf16[512,640]{1,0:T(8,128)(2,1)} custom-call(bf16[512,640]{1,0:T(8,128)(2,1)} %tokens.1, bf16[5120,640]{1,0:T(8,128)(2,1)} %w_query.1, bf16[5120,640]{1,0:T(8,128)(2,1)} %w_key.1, bf16[5120,640]{1,0:T(8,128)(2,1)} %w_value.1, bf16[4,128,640]{2,1,0:T(8,128)(2,1)} %cache_keys.1, bf16[4,128,640]{2,1,0:T(8,128)(2,1)} %cache_values.1, ...), custom_call_target="tpu_custom_call" | custom-call | tf_op jit(solution)/shard_map/pallas_call | solution.py:487
  79.2 2.0 %copy.10 = bf16[512,640]{1,0:T(8,128)(2,1)} copy(bf16[512,640]{1,0:T(8,128)(2,1)} %shard_map.82) | data formatting | bytes 1310720
